TPU v7x, 128 devices: a whole 4x4x4 slice. The times are simulated.
128 devices in a mesh: group: 4 (over y_hi, core), member: 32 (over z, y_lo, x).
Axes of the slice: x: 4, y: 4 (y_hi: 2, y_lo: 2; y = y_hi * 2 + y_lo), z: 4, core: 2. Of those that a mesh axis runs over, the one named last changes fastest.
Arguments:
- activations: bfloat16 [4096, 7, 7, 2048], P(('group', 'member')), may hold values from -24 to 24
- shuffle: int32 [4096], replicated, may hold values from 0 to 4095, as said below
- pointer: int32 [1], replicated, may hold values from 0 to 65535
- conv_reduce: bfloat16 [2048, 512], replicated, may hold values from -0.125 to 0.125
- conv_spatial: bfloat16 [3, 3, 512, 512], replicated, may hold values from -0.09375 to 0.09375
- conv_expand: bfloat16 [512, 2048], replicated, may hold values from -0.25 to 0.25
- key_head: bfloat16 [2048, 128], replicated, may hold values from -0.125 to 0.125
- queries: bfloat16 [4096, 128], P(('group', 'member')), may hold values from -6 to 6
- negative_memory: bfloat16 [65536, 128], P('member'), may hold values from -0.5 to 0.5
Outputs:
- logits: bfloat16 [4096, 65536], P('group', 'member')
- matching_pair_similarity: float32 [4096], P(('group', 'member'))
- new_queue: bfloat16 [65536, 128], P('member')
Inputs may be any that keep to these rules, and one draw needn't show every extreme that they name: `shuffle`: a permutation of 0 to 4095 that maps each aligned block of 1024 rows onto itself; the 32 rows of each device come from every device of that block, 1 row from each.
All inputs are finite; a program needn't handle non-finite values.
Results may differ from a plain program's by a relative error of at most 0.01.
Values may be sent and summed in bfloat16 or wider, within the bound.
No kernel may reach another device: no remote copies, remote signals or barrier semaphores. Data moves between devices by JAX's collectives and lax.ppermute only.
A program may use at most 128 MiB of HBM per device.

v0:
```python
import jax
import jax.numpy as jnp
from jax import lax
from jax.sharding import PartitionSpec as P

norm_eps = 1e-05
unit_eps = 1e-06
sharpness_divisor = 0.2


def local_moments(per_row):
    center = jnp.mean(per_row, axis=(0, 1), keepdims=True)
    spread = jnp.mean(per_row * per_row, axis=(0, 1), keepdims=True) - center * center
    return (center, spread)


def standardize(values, row_count, moments):
    per_row = values.reshape(row_count, 49, values.shape[1])
    center, spread = moments(per_row)
    return ((per_row - center) * lax.rsqrt(spread + norm_eps)).reshape(values.shape)


def encode(rows, conv_reduce, conv_spatial, conv_expand, key_head, moments):
    row_count = rows.shape[0]
    flat = rows.reshape(row_count * 49, rows.shape[3])
    first = jnp.dot(flat, conv_reduce, preferred_element_type=jnp.float32)
    reduced = jnp.maximum(standardize(first, row_count, moments), 0.0).astype(jnp.bfloat16)
    reduced = reduced.reshape(row_count, 7, 7, reduced.shape[1])
    padded = jnp.pad(reduced, ((0, 0), (1, 1), (1, 1), (0, 0)))
    second = jnp.zeros((row_count * 49, conv_spatial.shape[3]), jnp.float32)
    for shift_y in range(3):
        for shift_x in range(3):
            window = padded[:, shift_y : shift_y + 7, shift_x : shift_x + 7, :].reshape(
                row_count * 49, -1
            )
            second = second + jnp.dot(
                window, conv_spatial[shift_y, shift_x], preferred_element_type=jnp.float32
            )
    spatial = jnp.maximum(standardize(second, row_count, moments), 0.0).astype(jnp.bfloat16)
    third = jnp.dot(spatial, conv_expand, preferred_element_type=jnp.float32)
    merged = jnp.maximum(standardize(third, row_count, moments) + flat.astype(jnp.float32), 0.0)
    pooled = jnp.mean(merged.reshape(row_count, 49, -1), axis=1).astype(jnp.bfloat16)
    projected = jnp.dot(pooled, key_head, preferred_element_type=jnp.float32)
    return (
        projected * lax.rsqrt(jnp.sum(projected * projected, axis=1, keepdims=True) + unit_eps)
    ).astype(jnp.bfloat16)


def rank_within(bucket, order_value):
    same_bucket = bucket[:, None] == bucket[None, :]
    earlier = order_value[None, :] < order_value[:, None]
    return jnp.sum(jnp.logical_and(same_bucket, earlier), axis=1)


def per_device(
    activations,
    shuffle,
    pointer,
    conv_reduce,
    conv_spatial,
    conv_expand,
    key_head,
    queries,
    negative_memory,
):
    row_count = activations.shape[0]
    members = lax.axis_size("member")
    per_peer = row_count // members
    my_member = lax.axis_index("member")
    my_group = lax.axis_index("group")
    group_rows = members * row_count
    group_start = my_group * group_rows
    group_perm = lax.dynamic_slice_in_dim(shuffle, group_start, group_rows) - group_start
    row_ids = jnp.arange(row_count, dtype=jnp.int32)
    target = (
        jnp.zeros((group_rows,), jnp.int32)
        .at[group_perm]
        .set(jnp.arange(group_rows, dtype=jnp.int32))
    )
    my_start = my_member * row_count
    dest_member = lax.dynamic_slice_in_dim(target, my_start, row_count) // row_count
    send_slot = dest_member * per_peer + rank_within(dest_member, row_ids)
    send_order = jnp.zeros((row_count,), jnp.int32).at[send_slot].set(row_ids)
    outgoing = activations[send_order]
    incoming = lax.all_to_all(outgoing, "member", split_axis=0, concat_axis=0, tiled=True)
    sources = lax.dynamic_slice_in_dim(group_perm, my_start, row_count)
    source_member = sources // row_count
    recv_slot = source_member * per_peer + rank_within(source_member, sources)
    shuffled = incoming[recv_slot]
    mixed_keys = encode(shuffled, conv_reduce, conv_spatial, conv_expand, key_head, local_moments)
    placed = jnp.zeros_like(mixed_keys).at[recv_slot].set(mixed_keys)
    returned_rows = lax.all_to_all(placed, "member", split_axis=0, concat_axis=0, tiled=True)
    keys_restored = returned_rows[send_slot]
    query_f = queries.astype(jnp.float32)
    narrow_waist_layer = (
        query_f * lax.rsqrt(jnp.sum(query_f * query_f, axis=1, keepdims=True) + unit_eps)
    ).astype(jnp.bfloat16)
    similarity_matrix = (
        jnp.einsum(
            "qk,sk->qs",
            lax.all_gather(narrow_waist_layer, "member", axis=0, tiled=True),
            negative_memory,
            preferred_element_type=jnp.float32,
        )
        / sharpness_divisor
    )
    logits = similarity_matrix.astype(jnp.bfloat16)
    matching_pair_similarity = (
        jnp.sum(narrow_waist_layer.astype(jnp.float32) * keys_restored.astype(jnp.float32), axis=1)
        / sharpness_divisor
    )
    all_keys = lax.all_gather(keys_restored, ("group", "member"), axis=0, tiled=True)
    tile_rows = negative_memory.shape[0]
    total_slots = tile_rows * members
    batch_rows = all_keys.shape[0]
    slot_ids = my_member * tile_rows + jnp.arange(tile_rows, dtype=jnp.int32)
    offset = jnp.mod(slot_ids - pointer[0], total_slots)
    fresh = all_keys[jnp.minimum(offset, batch_rows - 1)]
    new_queue = jnp.where((offset < batch_rows)[:, None], fresh, negative_memory)
    return (logits, matching_pair_similarity, new_queue)


def solution(mesh):
    placed = (
        P(("group", "member"), None, None, None),
        P(),
        P(),
        P(),
        P(),
        P(),
        P(),
        P(("group", "member"), None),
        P("member", None),
    )
    return jax.shard_map(
        per_device,
        mesh=mesh,
        in_specs=placed,
        out_specs=(P("group", "member"), P(("group", "member")), P("member", None)),
        check_vma=False,
    )
```

profile of v0, /device:TPU:1, one launch (start us, length us, event | category | flops | bytes accessed | tf_op | source)
XLA Modules:
  0.0 609.8 jit_solution(14537643689102882550)
XLA Ops:
  8.0 4.3 scatter_custom_fusion
  13.3 17.5 %gather_fusion = bf16[32,7,7,2048]{3,0,2,1:T(8,128)(2,1)} fusion(bf16[32,7,7,2048]{3,0,2,1:T(8,128)(2,1)} %param.9, s32[1024]{0:T(1024)S(1)} %pad_clamp_fusion.2), kind=kCustom, calls=%fused_computation | custom fusion | bytes 12845184 | tf_op jit(solution)/shard_map/gather | solution.py:84
  30.8 9.8 %copy.53 = bf16[32,7,7,2048]{3,2,1,0:T(8,128)(2,1)} copy(bf16[32,7,7,2048]{3,0,2,1:T(8,128)(2,1)} %gather_fusion) | data formatting | bytes 12845056 | tf_op jit(solution)/shard_map/gather | solution.py:84
  40.6 9.8 %all-to-all-start = ((bf16[32,7,7,2048]{3,2,1,0:T(8,128)(2,1)}), bf16[32,7,7,2048]{3,2,1,0:T(8,128)(2,1)}, u32[]{:S(2)}, u32[]{:S(2)}) async-start(bf16[32,7,7,2048]{3,2,1,0:T(8,128)(2,1)} %copy.53), calls=%async_computation | async-start | bytes 14680064 | tf_op jit(solution)/shard_map/all_to_all | solution.py:85
  50.6 100.8 %all-to-all-done = bf16[32,7,7,2048]{3,2,1,0:T(8,128)(2,1)} async-done(((bf16[32,7,7,2048]{3,2,1,0:T(8,128)(2,1)}), bf16[32,7,7,2048]{3,2,1,0:T(8,128)(2,1)}, u32[]{:S(2)}, u32[]{:S(2)}) %all-to-all-start) | async-done | bytes 6422560 | tf_op jit(solution)/shard_map/all_to_all | solution.py:85
  151.4 7.1 %gather_fusion.1 = bf16[32,7,7,2048]{3,2,1,0:T(8,128)(2,1)} fusion(bf16[32,7,7,2048]{3,2,1,0:T(8,128)(2,1)} %all-to-all-done, s32[1024]{0:T(1024)S(1)} %pad_clamp_fusion.1), kind=kCustom, calls=%fused_computation.1 | custom fusion | bytes 12845184 | tf_op jit(solution)/shard_map/gather | solution.py:89
  158.5 7.3 %copy.54 = bf16[32,7,7,2048]{3,0,2,1:T(8,128)(2,1)S(1)} copy(bf16[32,7,7,2048]{3,2,1,0:T(8,128)(2,1)} %gather_fusion.1) | data formatting | bytes 12845056 | tf_op jit(solution)/shard_map/gather | solution.py:89
  165.9 6.0 fusion.42
  178.3 5.2 pad_slice_fusion
  185.6 3.7 reshape.190
  189.3 3.5 copy.58
  192.9 3.7 reshape.184
  196.6 3.5 copy.59
  200.1 3.7 reshape.185
  203.8 3.5 copy.60
  207.4 3.7 reshape.186
  211.1 3.5 copy.61
  214.6 3.7 reshape.187
  218.3 3.5 copy.62
  221.9 3.7 reshape.188
  225.6 3.5 copy.63
  229.1 3.7 reshape.189
  232.8 3.5 copy.57
  236.4 3.9 reshape.183
  259.2 9.0 %fusion.41 = (f32[2048]{0:T(1024)S(1)}, f32[2048]{0:T(1024)S(1)}, f32[32,49,2048]{2,1,0:T(8,128)}) fusion(bf16[32,49,512]{2,1,0:T(8,128)(2,1)} %dot_general.55, bf16[512,2048]{1,0:T(8,128)(2,1)S(1)} %copy-done), kind=kOutput, calls=%fused_computation.115 | convolution fusion | flops 3297964032 | bytes 16564224 | tf_op jit(solution)/shard_map/dot_general | solution.py:40
  268.3 12.7 %maximum_reduce_fusion = f32[32,2048]{1,0:T(8,128)S(1)} fusion(f32[32,49,2048]{2,1,0:T(8,128)} %get-tuple-element.31, f32[2048]{0:T(1024)S(1)} %get-tuple-element.24, f32[2048]{0:T(1024)S(1)} %get-tuple-element.23, bf16[32,49,2048]{2,0,1:T(8,128)(2,1)} %bitcast.66), kind=kLoop, calls=%fused_computation.7 | loop fusion | flops 19202048 | bytes 19546112 | tf_op jit(solution)/shard_map/reduce_sum | solution.py:42
  282.7 9.3 %all-to-all-start.1 = ((bf16[32,1,128]{2,1,0:T(2,128)(2,1)}), bf16[32,1,128]{2,1,0:T(2,128)(2,1)S(1)}, u32[]{:S(2)}, u32[]{:S(2)}) async-start(bf16[32,1,128]{2,1,0:T(2,128)(2,1)} %copy.66), calls=%async_computation.1 | async-start | bytes 32768 | tf_op jit(solution)/shard_map/all_to_all | solution.py:92
  292.0 7.0 %all-to-all-done.1 = bf16[32,1,128]{2,1,0:T(2,128)(2,1)S(1)} async-done(((bf16[32,1,128]{2,1,0:T(2,128)(2,1)}), bf16[32,1,128]{2,1,0:T(2,128)(2,1)S(1)}, u32[]{:S(2)}, u32[]{:S(2)}) %all-to-all-start.1) | async-done | bytes 8224 | tf_op jit(solution)/shard_map/all_to_all | solution.py:92
  302.0 64.2 %all_gather.6 = bf16[1024,128]{1,0:T(8,128)(2,1)S(1)} all-gather(bf16[32,128]{1,0:T(8,128)(2,1)S(1)} %get-tuple-element.10), channel_id=1, replica_groups=mesh['group'=4,'member'=32] {'member'}, dimensions={0}, use_global_device_ids=true | all-gather | bytes 270336 | tf_op jit(solution)/shard_map/all_gather | solution.py:101
  366.7 3.3 multiply_convert_fusion
  369.9 224.5 %all-gather.3.cloned.1.call-done = bf16[4096,128]{1,0:T(8,128)(2,1)} async-done(((bf16[32,128]{1,0:T(8,128)(2,1)}), bf16[4096,128]{1,0:T(8,128)(2,1)}) %all-gather.3.cloned.1.call-update) | async-done | bytes 1048592 | tf_op jit(solution)/shard_map/all_gather | solution.py:112
  594.4 7.0 %gather_fusion.3 = bf16[2048,128]{1,0:T(8,128)(2,1)S(1)} fusion(bf16[4096,128]{1,0:T(8,128)(2,1)} %all-gather.3.cloned.1.call-done, s32[2048]{0:T(1024)S(1)} %broadcast_clamp_fusion), kind=kCustom, calls=%fused_computation.3 | custom fusion | bytes 1056768 | tf_op jit(solution)/shard_map/gather | solution.py:118
  (80 shorter events, 35.0 us)
Async XLA Ops:
  7.2 252.0 %copy-start = (bf16[512,2048]{1,0:T(8,128)(2,1)S(1)}, bf16[512,2048]{1,0:T(8,128)(2,1)}, u32[]{:S(2)}) copy-start(bf16[512,2048]{1,0:T(8,128)(2,1)} %param.14) | copy-start | bytes 6291460
  40.6 110.8 %all-to-all-start = ((bf16[32,7,7,2048]{3,2,1,0:T(8,128)(2,1)}), bf16[32,7,7,2048]{3,2,1,0:T(8,128)(2,1)}, u32[]{:S(2)}, u32[]{:S(2)}) async-start(bf16[32,7,7,2048]{3,2,1,0:T(8,128)(2,1)} %copy.53), calls=%async_computation | async-start | bytes 14680064 | tf_op jit(solution)/shard_map/all_to_all | solution.py:85
  158.5 7.4 %copy-start.13 = (bf16[2048,512]{1,0:T(8,128)(2,1)S(1)}, bf16[2048,512]{1,0:T(8,128)(2,1)}, u32[]{:S(2)}) copy-start(bf16[2048,512]{1,0:T(8,128)(2,1)} %param.12) | copy-start | bytes 6291460
  165.9 6.0 copy-start.1
  240.3 2.7 copy-start.4
  240.3 4.9 slice-start
  243.0 2.2 copy-start.6
  243.0 2.2 slice-start.1
  245.2 1.4 copy-start.8
  246.7 1.4 copy-start.3
  248.1 1.4 copy-start.5
  249.5 1.4 copy-start.7
  250.9 1.4 copy-start.9
  252.3 1.4 copy-start.2
  268.2 12.8 %copy-start.11 = (bf16[2048,128]{1,0:T(8,128)(2,1)S(1)}, bf16[2048,128]{1,0:T(8,128)(2,1)}, u32[]{:S(2)}) copy-start(bf16[2048,128]{1,0:T(8,128)(2,1)} %param.15) | copy-start | bytes 1572868
  268.2 32.7 %copy-start.12 = (bf16[32,128]{1,0:T(8,128)(2,1)S(1)}, bf16[32,128]{1,0:T(8,128)(2,1)}, u32[]{:S(2)}) copy-start(bf16[32,128]{1,0:T(8,128)(2,1)} %param.16) | copy-start | bytes 24580
  268.2 98.4 %copy-start.10 = (bf16[2048,128]{1,0:T(8,128)(2,1)S(1)}, bf16[2048,128]{1,0:T(8,128)(2,1)}, u32[]{:S(2)}) copy-start(bf16[2048,128]{1,0:T(8,128)(2,1)} %param.17) | copy-start | bytes 1572868
  282.7 16.3 %all-to-all-start.1 = ((bf16[32,1,128]{2,1,0:T(2,128)(2,1)}), bf16[32,1,128]{2,1,0:T(2,128)(2,1)S(1)}, u32[]{:S(2)}, u32[]{:S(2)}) async-start(bf16[32,1,128]{2,1,0:T(2,128)(2,1)} %copy.66), calls=%async_computation.1 | async-start | bytes 32768 | tf_op jit(solution)/shard_map/all_to_all | solution.py:92
  291.9 302.5 %all-gather.3.cloned.1.call-start = ((), (), s32[]{:S(2)}) async-start(), calls=%async_computation.2 | async-start | bytes 1056768 | tf_op jit(solution)/shard_map/all_gather | solution.py:112
Sparse Core Ops, SparseCore 0:
  300.3 294.0 all-gather.2
where the time goes:
time: 621 us; the launch traced here: 610 us
  waiting for transfers between devices  332 us (53%)
  local copies, waits for them, and re-layouts  127 us (20%)
  blocking collectives  64.2 us (10%)
  matrix products  30.5 us (5%)
  other arithmetic  21 us (3%)
  starting transfers between devices  19.1 us (3%)
  between operations  15.5 us (2%)
    all_gather x1, waiting for transfers between devices, per_device(): lax.all_gather(keys_restored, ('group', 'member'), axis=0, tiled=True)  224 us
    all_to_all x1, waiting for transfers between devices, per_device(): lax.all_to_all(outgoing, 'member', split_axis=0, concat_axis=0, tiled=True)  101 us
    all_gather x1, blocking collectives, per_device(): lax.all_gather(narrow_waist_layer, 'member', axis=0, tiled=True)  64.2 us
    slice x9, local copies, waits for them, and re-layouts, encode(): padded[:, shift_y:shift_y + 7, shift_x:shift_x + 7, :]  32.1 us
    reshape x8, local copies, waits for them, and re-layouts, encode(): padded[:, shift_y:shift_y + 7, shift_x:shift_x + 7, :]  29.9 us
    gather x2, local copies, waits for them, and re-layouts, per_device(): outgoing = activations[send_order]  27.2 us
    gather x2, local copies, waits for them, and re-layouts, per_device(): shuffled = incoming[recv_slot]  14.5 us
    reduce_sum x1, other arithmetic, encode(): jnp.mean(merged.reshape(row_count, 49, -1), axis=1).astype(jnp.bfloat16)  12.7 us
  transfers between devices with their start and end apart: 3, of which 3 were waited for; matrix products, arithmetic and copies ran while one was open for 1% of the time, Pallas kernels for 0%

commit v1 on v0

v1 whole, which is shorter than its diff:
```python
import jax
import jax.numpy as jnp
from jax import lax
from jax.experimental import pallas as pl
from jax.experimental.pallas import tpu as pltpu
from jax.sharding import PartitionSpec as P

norm_eps = 1e-05
unit_eps = 1e-06
sharpness_divisor = 0.2

IMAGES = 32
SIDE = 7
POSITIONS = SIDE * SIDE
ROW = SIDE * IMAGES
ROWS = POSITIONS * IMAGES
MID = 512
OUT = 2048
KEY = 128
SLAB = 16
MIB = 1 << 20
f32 = jnp.float32
bf16 = jnp.bfloat16


def iota(shape, dim):
    return lax.broadcasted_iota(jnp.int32, shape, dim)


def dot(a, b):
    return jnp.dot(a, b, preferred_element_type=f32)


def dot_tn(a, b):
    return lax.dot_general(a, b, (((0,), (0,)), ((), ())), preferred_element_type=f32)


def dot_nt(a, b):
    return lax.dot_general(a, b, (((1,), (1,)), ((), ())), preferred_element_type=f32)


def spread_select(select):
    size = IMAGES * SLAB
    left = (iota((size, IMAGES), 0) // SLAB == iota((size, IMAGES), 1)).astype(bf16)
    right = (iota((IMAGES, size), 0) == iota((IMAGES, size), 1) % IMAGES).astype(bf16)
    spread = dot(dot(left, select).astype(bf16), right)
    same = iota((size, size), 0) % SLAB == iota((size, size), 1) // IMAGES
    return jnp.where(same, spread, 0.0).astype(bf16)


def split(value):
    high = value.astype(bf16)
    return high, (value - high.astype(f32)).astype(bf16)


def unit_of(queries):
    query_f = queries.astype(f32)
    return query_f * lax.rsqrt(jnp.sum(query_f * query_f, axis=1, keepdims=True) + unit_eps)


def reduce_kernel(
    place_ref, x_ref, weight_ref, table_ref, query_ref,
    delta_ref, mean_ref, select_ref, message_ref, first, total,
):
    step = pl.program_id(0)
    part = dot(x_ref[...], weight_ref[...])
    first[pl.ds(pl.multiple_of(step * ROW, ROW), ROW), :] = part
    image_sum = jnp.sum(part.reshape(SIDE, IMAGES, MID), axis=0)

    @pl.when(step == 0)
    def _():
        total[...] = image_sum

    @pl.when(step > 0)
    def _():
        total[...] += image_sum

    @pl.when(step == SIDE - 1)
    def _():
        mean = (total[...] * (1.0 / POSITIONS)).astype(bf16)
        mean_f = mean.astype(f32)
        mean_ref[...] = mean
        for y in range(SIDE):
            rows = pl.ds(y * ROW, ROW)
            centered = first[rows, :].reshape(SIDE, IMAGES, MID) - mean_f[None]
            delta_ref[rows, :] = centered.reshape(ROW, MID).astype(bf16)
        table = table_ref[pl.ds(pl.multiple_of(place_ref[0] * IMAGES, IMAGES), IMAGES), :]
        local = table - (place_ref[0] * (IMAGES * IMAGES) + place_ref[1] * IMAGES)
        mine = jnp.logical_and(local >= 0, local < IMAGES)
        chosen = jnp.sum(jnp.where(mine, local, 0), axis=1, keepdims=True)
        select = (chosen == iota((IMAGES, IMAGES), 1)).astype(bf16)
        select_ref[...] = select
        mover = spread_select(select)
        size = SLAB * IMAGES
        for slab in range(3):
            moved = dot(mover, delta_ref[pl.ds(slab * size, size), :])
            message_ref[:, pl.ds(slab * SLAB, SLAB), :] = moved.reshape(IMAGES, SLAB, MID).astype(bf16)
        last = jnp.concatenate([delta_ref[pl.ds(3 * size, IMAGES), :], mean], axis=0)
        moved = dot(mover[:, : 2 * IMAGES], last).reshape(IMAGES, SLAB, MID)
        unit = unit_of(query_ref[...])
        unit = jnp.concatenate([unit[8 * k : 8 * k + 8] for k in range(4)], axis=1)
        moved = jnp.concatenate(
            [moved[:, :8, :], jnp.broadcast_to(unit[None], (IMAGES, 8, MID))], axis=1
        )
        message_ref[:, pl.ds(3 * SLAB, SLAB), :] = moved.astype(bf16)


def store_windows(windows, reduced, y):
    edge = jnp.zeros((IMAGES, MID), bf16)
    at = (y + 1) * ROW
    windows[pl.ds(at, IMAGES), pl.ds(0, MID)] = edge
    windows[pl.ds(at + IMAGES, ROW - IMAGES), pl.ds(0, MID)] = reduced[: ROW - IMAGES]
    windows[pl.ds(at, ROW), pl.ds(MID, MID)] = reduced
    windows[pl.ds(at, ROW - IMAGES), pl.ds(2 * MID, MID)] = reduced[IMAGES:]
    windows[pl.ds(at + ROW - IMAGES, IMAGES), pl.ds(2 * MID, MID)] = edge


def clear_border(windows):
    border = jnp.zeros((ROW, 3 * MID), bf16)
    windows[pl.ds(0, ROW), :] = border
    windows[pl.ds((SIDE + 1) * ROW, ROW), :] = border


def convolve_row(windows, spatial_weight, y):
    return (
        dot(windows[pl.ds(y * ROW, ROW), :], spatial_weight[0])
        + dot(windows[pl.ds((y + 1) * ROW, ROW), :], spatial_weight[1])
        + dot(windows[pl.ds((y + 2) * ROW, ROW), :], spatial_weight[2])
    )


def fold(value):
    return jnp.sum(value.reshape(-1, IMAGES, value.shape[1]), axis=0)


def centered_spread(values, center):
    total = jnp.zeros((IMAGES, values.shape[1]), f32)
    for y in range(SIDE):
        away = values[pl.ds(y * ROW, ROW), :] - center
        total = total + fold(away * away)
    return jnp.sum(total, axis=0, keepdims=True) * (1.0 / ROWS)


def block_kernel(
    received_ref, spatial_hbm, expand_hbm, message_ref, units_ref,
    values, windows, spatial, spatial_weight, expand_weight, sems,
):
    load_spatial = pltpu.make_async_copy(spatial_hbm, spatial_weight, sems.at[0])
    load_expand = pltpu.make_async_copy(expand_hbm, expand_weight, sems.at[1])
    load_spatial.start()
    load_expand.start()

    size = SLAB * IMAGES
    row, column = iota((size, size), 0), iota((size, size), 1)
    mover = jnp.logical_and(row % IMAGES == column // SLAB, row // IMAGES == column % SLAB).astype(bf16)
    tail = received_ref[:, pl.ds(3 * SLAB, SLAB), :]
    last = dot(mover[: 2 * IMAGES], tail.reshape(size, MID))
    mean = last[IMAGES:]
    total = jnp.zeros((IMAGES, MID), f32)
    for slab in range(3):
        moved = dot(mover, received_ref[:, pl.ds(slab * SLAB, SLAB), :].reshape(size, MID))
        moved = (moved.reshape(SLAB, IMAGES, MID) + mean[None]).reshape(size, MID)
        values[pl.ds(slab * size, size), :] = moved
        total = total + fold(moved)
    values[pl.ds(3 * size, IMAGES), :] = last[:IMAGES] + mean
    total = total + last[:IMAGES] + mean

    units = tail.astype(f32)[:, 8:, :]
    units = jnp.concatenate(
        [units[:, None, :, k * KEY : (k + 1) * KEY] for k in range(4)], axis=1
    )
    units_ref[...] = units.reshape(IMAGES * IMAGES, KEY).astype(bf16)

    center1 = jnp.sum(total, axis=0, keepdims=True) * (1.0 / ROWS)
    scale1 = lax.rsqrt(centered_spread(values, center1) + norm_eps)
    clear_border(windows)
    for y in range(SIDE):
        reduced = jnp.maximum((values[pl.ds(y * ROW, ROW), :] - center1) * scale1, 0.0)
        store_windows(windows, reduced.astype(bf16), y)

    load_spatial.wait()
    total = jnp.zeros((IMAGES, MID), f32)
    for y in range(SIDE):
        second = convolve_row(windows, spatial_weight, y)
        values[pl.ds(y * ROW, ROW), :] = second
        total = total + fold(second)
    center2 = jnp.sum(total, axis=0, keepdims=True) * (1.0 / ROWS)
    scale2 = lax.rsqrt(centered_spread(values, center2) + norm_eps)
    total = jnp.zeros((IMAGES, MID), f32)
    for y in range(SIDE):
        rows = pl.ds(y * ROW, ROW)
        kept = jnp.maximum((values[rows, :] - center2) * scale2, 0.0).astype(bf16)
        spatial[rows, :] = kept
        total = total + fold(kept.astype(f32))
    spatial_mean = jnp.sum(total, axis=0, keepdims=True) * (1.0 / ROWS)

    load_expand.wait()
    scale3 = []
    for part in range(OUT // MID):
        columns = pl.ds(part * MID, MID)
        total = jnp.zeros((IMAGES, MID), f32)
        for y in range(SIDE):
            third = dot(spatial[pl.ds(y * ROW, ROW), :], expand_weight[:, columns])
            values[pl.ds(y * ROW, ROW), :] = third
            total = total + fold(third)
        center3 = jnp.sum(total, axis=0, keepdims=True) * (1.0 / ROWS)
        scale3.append(lax.rsqrt(centered_spread(values, center3) + norm_eps))

    parts = []
    for value in (center1, scale1, center2, scale2, spatial_mean):
        parts += [piece.astype(f32) for piece in split(value)]
    parts += scale3
    parts.append(jnp.zeros((SLAB - len(parts), MID), f32))
    message = jnp.concatenate(parts, axis=0)
    message_ref[...] = jnp.broadcast_to(message[None], (IMAGES, SLAB, MID)).astype(bf16)


def home_kernel(
    received_ref, select_ref, delta_ref, mean_ref, query_ref, head_ref, x_hbm, spatial_hbm, expand_hbm,
    key_ref, similarity_ref,
    windows, x, spatial, spatial_weight, expand_weight, pooled, sems,
):
    load_spatial = pltpu.make_async_copy(spatial_hbm, spatial_weight, sems.at[0])
    load_expand = pltpu.make_async_copy(expand_hbm, expand_weight, sems.at[1])
    load_x = pltpu.make_async_copy(x_hbm, x, sems.at[2])
    load_spatial.start()
    load_expand.start()
    load_x.start()

    size = SLAB * IMAGES
    mover = spread_select(select_ref[...])
    stats = dot_tn(mover, received_ref[...].reshape(size, MID)).reshape(SLAB, IMAGES, MID)
    offset1 = mean_ref[...].astype(f32) - (stats[0] + stats[1])
    scale1 = stats[2] + stats[3]
    center2 = stats[4] + stats[5]
    scale2 = stats[6] + stats[7]
    mean_high, mean_low = stats[8].astype(bf16), stats[9].astype(bf16)

    clear_border(windows)
    for y in range(SIDE):
        delta = delta_ref[pl.ds(y * ROW, ROW), :].astype(f32).reshape(SIDE, IMAGES, MID)
        reduced = jnp.maximum((delta + offset1[None]) * scale1[None], 0.0)
        store_windows(windows, reduced.reshape(ROW, MID).astype(bf16), y)

    load_spatial.wait()
    for y in range(SIDE):
        second = convolve_row(windows, spatial_weight, y).reshape(SIDE, IMAGES, MID)
        kept = jnp.maximum((second - center2[None]) * scale2[None], 0.0)
        spatial[pl.ds(y * ROW, ROW), :] = kept.reshape(ROW, MID).astype(bf16)

    load_expand.wait()
    load_x.wait()
    for part in range(OUT // MID):
        columns = pl.ds(part * MID, MID)
        weight = expand_weight[:, columns]
        center3 = dot(mean_high, weight) + dot(mean_low, weight)
        scale3 = stats[10 + part]
        total = jnp.zeros((IMAGES, MID), f32)
        for y in range(SIDE):
            rows = pl.ds(y * ROW, ROW)
            third = dot(spatial[rows, :], weight).reshape(SIDE, IMAGES, MID)
            kept = x[rows, columns].astype(f32).reshape(SIDE, IMAGES, MID)
            merged = jnp.maximum((third - center3[None]) * scale3[None] + kept, 0.0)
            total = total + jnp.sum(merged, axis=0)
        pooled[:, columns] = (total * (1.0 / POSITIONS)).astype(bf16)
    projected = dot(pooled[...], head_ref[...])
    key = projected * lax.rsqrt(jnp.sum(projected * projected, axis=1, keepdims=True) + unit_eps)
    key = key.astype(bf16)
    unit = unit_of(query_ref[...]).astype(bf16)
    pairs = dot_nt(unit, key)
    own = iota((IMAGES, IMAGES), 0) == iota((IMAGES, IMAGES), 1)
    similarity_ref[...] = jnp.sum(jnp.where(own, pairs, 0.0), axis=0, keepdims=True) / sharpness_divisor
    key_ref[...] = jnp.broadcast_to(key[None], key_ref.shape)


def queue_kernel(place_ref, near_ref, far_ref, memory_ref, out_ref, padded):
    slots = memory_ref.shape[0]
    batch = IMAGES * 128
    core = place_ref[2]
    start = place_ref[3]
    edge = jnp.zeros((slots, KEY), bf16)
    padded[pl.ds(0, slots), :] = edge
    padded[pl.ds(slots + batch, slots), :] = edge
    padded[pl.ds(2 * slots + batch, SLAB), :] = edge[:SLAB]
    half = IMAGES * IMAGES
    for high in range(2):
        for ref, which in ((near_ref, core), (far_ref, 1 - core)):
            at = pl.multiple_of(slots + (2 * high + which) * half, half)
            padded[pl.ds(at, half), :] = ref[pl.ds(high * IMAGES, IMAGES)].reshape(half, KEY)
    tile = 256
    base = start // SLAB * SLAB
    inner = start - base
    pick = (iota((tile, tile + SLAB), 1) == iota((tile, tile + SLAB), 0) + inner).astype(bf16)
    for part in range(slots // tile):
        rows = padded[pl.ds(pl.multiple_of(base + part * tile, SLAB), tile + SLAB), :]
        fresh = dot(pick, rows)
        index = start - slots + part * tile + iota((tile, KEY), 0)
        inside = jnp.logical_and(index >= 0, index < batch)
        old = memory_ref[pl.ds(part * tile, tile), :].astype(f32)
        out_ref[pl.ds(part * tile, tile), :] = jnp.where(inside, fresh, old).astype(bf16)


def params(mib):
    return pltpu.CompilerParams(vmem_limit_bytes=mib * MIB)


VMEM = pl.BlockSpec(memory_space=pltpu.VMEM)
SMEM = pl.BlockSpec(memory_space=pltpu.SMEM)
HBM = pl.BlockSpec(memory_space=pl.ANY)


def shape(*dims, dtype=bf16):
    return jax.ShapeDtypeStruct(dims, dtype)


def reduce_call(place, x, conv_reduce, table, queries):
    whole = lambda dims: pl.BlockSpec(dims, lambda step: (0,) * len(dims))
    return pl.pallas_call(
        reduce_kernel,
        grid=(SIDE,),
        in_specs=[
            SMEM,
            pl.BlockSpec((ROW, OUT), lambda step: (step, 0)),
            whole((OUT, MID)),
            whole(table.shape),
            whole((IMAGES, KEY)),
        ],
        out_specs=[
            whole((ROWS, MID)),
            whole((IMAGES, MID)),
            whole((IMAGES, IMAGES)),
            whole((IMAGES, 4 * SLAB, MID)),
        ],
        out_shape=[
            shape(ROWS, MID),
            shape(IMAGES, MID),
            shape(IMAGES, IMAGES),
            shape(IMAGES, 4 * SLAB, MID),
        ],
        scratch_shapes=[pltpu.VMEM((ROWS, MID), f32), pltpu.VMEM((IMAGES, MID), f32)],
        compiler_params=params(40),
        name="reduce",
    )(place, x, conv_reduce, table, queries)


def block_call(received, conv_spatial, conv_expand):
    return pl.pallas_call(
        block_kernel,
        in_specs=[VMEM, HBM, HBM],
        out_specs=[VMEM, VMEM],
        out_shape=[shape(IMAGES, SLAB, MID), shape(IMAGES * IMAGES, KEY)],
        scratch_shapes=[
            pltpu.VMEM((ROWS, MID), f32),
            pltpu.VMEM((ROWS + 2 * ROW, 3 * MID), bf16),
            pltpu.VMEM((ROWS, MID), bf16),
            pltpu.VMEM((3, 3 * MID, MID), bf16),
            pltpu.VMEM((MID, OUT), bf16),
            pltpu.SemaphoreType.DMA((2,)),
        ],
        compiler_params=params(48),
        name="block",
    )(received, conv_spatial, conv_expand)


def home_call(received, select, delta, mean, queries, key_head, x, conv_spatial, conv_expand, copies):
    return pl.pallas_call(
        home_kernel,
        in_specs=[VMEM] * 6 + [HBM] * 3,
        out_specs=[VMEM, VMEM],
        out_shape=[shape(copies, IMAGES, KEY), shape(1, IMAGES, dtype=f32)],
        scratch_shapes=[
            pltpu.VMEM((ROWS + 2 * ROW, 3 * MID), bf16),
            pltpu.VMEM((ROWS, OUT), bf16),
            pltpu.VMEM((ROWS, MID), bf16),
            pltpu.VMEM((3, 3 * MID, MID), bf16),
            pltpu.VMEM((MID, OUT), bf16),
            pltpu.VMEM((IMAGES, OUT), bf16),
            pltpu.SemaphoreType.DMA((3,)),
        ],
        compiler_params=params(48),
        name="home",
    )(received, select, delta, mean, queries, key_head, x, conv_spatial, conv_expand)


def queue_call(place, near, far, memory):
    return pl.pallas_call(
        queue_kernel,
        in_specs=[SMEM] + [VMEM] * 3,
        out_specs=VMEM,
        out_shape=shape(*memory.shape),
        scratch_shapes=[pltpu.VMEM((2 * memory.shape[0] + IMAGES * 128 + SLAB, KEY), bf16)],
        compiler_params=params(32),
        name="queue",
    )(place, near, far, memory)


def per_device(
    activations, shuffle, pointer, conv_reduce, conv_spatial, conv_expand, key_head, queries, negative_memory
):
    group, member = lax.axis_index("group"), lax.axis_index("member")
    members = lax.axis_size("member")
    slots = negative_memory.shape[0]
    total_slots = slots * members
    batch = shuffle.shape[0]
    offset = jnp.mod(member * slots - pointer[0], total_slots)
    wrapped = jnp.where(offset > total_slots - slots, offset - total_slots, batch)
    start = slots + jnp.where(offset < batch, offset, wrapped)
    place = jnp.stack([group, member, group % 2, start]).astype(jnp.int32)

    x = activations.transpose(1, 2, 0, 3).reshape(ROWS, OUT)
    spatial_weight = conv_spatial.reshape(3, 3 * MID, MID)
    table = shuffle.reshape(batch // IMAGES, IMAGES)
    delta, mean, select, message = reduce_call(place, x, conv_reduce, table, queries)
    received = lax.all_to_all(message, "member", split_axis=0, concat_axis=0, tiled=True)
    moments, units = block_call(received, spatial_weight, conv_expand)
    returned = lax.all_to_all(moments, "member", split_axis=0, concat_axis=0, tiled=True)
    logits = (dot_nt(units, negative_memory) / sharpness_divisor).astype(bf16)
    copies, similarity = home_call(
        returned, select, delta, mean, queries, key_head, x, spatial_weight, conv_expand, 2 * members
    )
    same_core = [[g * members + m for g in (core, core + 2) for m in range(members)] for core in (0, 1)]
    near = lax.all_to_all(
        copies, ("group", "member"), split_axis=0, concat_axis=0, tiled=True, axis_index_groups=same_core
    )
    far = lax.ppermute(near, "group", [(0, 1), (1, 0), (2, 3), (3, 2)])
    new_queue = queue_call(place, near, far, negative_memory)
    return logits, similarity.reshape(IMAGES), new_queue


def solution(mesh):
    placed = (
        P(("group", "member"), None, None, None),
        P(),
        P(),
        P(),
        P(),
        P(),
        P(),
        P(("group", "member"), None),
        P("member", None),
    )
    return jax.shard_map(
        per_device,
        mesh=mesh,
        in_specs=placed,
        out_specs=(P("group", "member"), P(("group", "member")), P("member", None)),
        check_vma=False,
    )
```

time: 621 us -> 125 us (0.20); the launches traced: 610 us -> 124 us
  waiting for transfers between devices: 332 us -> 0.01 us
  local copies, waits for them, and re-layouts: 127 us -> 5.92 us
  Pallas kernels: 0 us -> 40.8 us
  matrix products: 30.5 us -> 3.27 us
  other arithmetic: 21 us -> 0.08 us
  starting transfers between devices: 19.1 us -> 3.74 us
  between operations: 15.5 us -> 1.35 us
    all_gather x1 -> x0, waiting for transfers between devices: 224 us -> none  [per_device(): lax.all_gather(keys_restored, ('group', 'member'), axis=0, tiled=True)]
    all_to_all x2 -> x0, waiting for transfers between devices: 108 us -> none  [the longest x1 101 us: per_device(): lax.all_to_all(outgoing, 'member', split_axis=0, concat_axis=0, tiled=True)]
    all_to_all x0 -> x3, blocking collectives: none -> 69.1 us  [the longest x1 36.3 us: per_device(): lax.all_to_all(message, 'member', split_axis=0, concat_axis=0, tiled=True)]
    all_gather x1 -> x0, blocking collectives: 64.2 us -> none  [per_device(): lax.all_gather(narrow_waist_layer, 'member', axis=0, tiled=True)]
    gather x6 -> x0, local copies, waits for them, and re-layouts: 49.9 us -> none  [the longest x2 27.2 us: per_device(): outgoing = activations[send_order]]
    pallas_call x0 -> x4, Pallas kernels: none -> 40.8 us  [the longest x1 16.2 us: block_call(): pl.pallas_call(block_kernel, in_specs=[VMEM, HBM, HBM], out_specs=[VMEM,...]
    slice x9 -> x0, local copies, waits for them, and re-layouts: 32.1 us -> none  [encode(): padded[:, shift_y:shift_y + 7, shift_x:shift_x + 7, :]]
    reshape x8 -> x1, local copies, waits for them, and re-layouts: 29.9 us -> 0.79 us  [per_device(): table = shuffle.reshape(batch // IMAGES, IMAGES)]
  transfers between devices with their start and end apart: 3 -> 1, of which waited for: 3 -> 0; matrix products, arithmetic and copies ran while one was open for 1% -> 3% of each run, Pallas kernels for 0% -> 0%
where the time goes in v1:
time: 125 us; the launch traced here: 124 us
  blocking collectives  69.1 us (55%)
  Pallas kernels  40.8 us (33%)
  local copies, waits for them, and re-layouts  5.92 us (5%)
  starting transfers between devices  3.74 us (3%)
  matrix products  3.27 us (3%)
  between operations  1.35 us (1%)
    all_to_all x1, blocking collectives, per_device(): lax.all_to_all(message, 'member', split_axis=0, concat_axis=0, tiled=True)  36.3 us
    all_to_all x1, blocking collectives, per_device(): lax.all_to_all(copies, ('group', 'member'), split_axis=0, concat_axis=0,...  17.9 us
    pallas_call x1, Pallas kernels, block_call(): pl.pallas_call(block_kernel, in_specs=[VMEM, HBM, HBM], out_specs=[VMEM,...  16.2 us
    pallas_call x1, Pallas kernels, home_call(): pl.pallas_call(home_kernel, in_specs=[VMEM] * 6 + [HBM] * 3, out_specs=[V...  15.8 us
    all_to_all x1, blocking collectives, per_device(): lax.all_to_all(moments, 'member', split_axis=0, concat_axis=0, tiled=True)  14.9 us
    pallas_call x1, Pallas kernels, reduce_call(): pl.pallas_call(reduce_kernel, grid=(SIDE,), in_specs=[SMEM, pl.BlockSpec(...  6.63 us
    unnamed x14, local copies, waits for them, and re-layouts  5.13 us
    ppermute x1, starting transfers between devices, per_device(): far = lax.ppermute(near, 'group', [(0, 1), (1, 0), (2, 3), (3, 2)])  3.74 us
  transfers between devices with their start and end apart: 1, of which 0 were waited for; matrix products, arithmetic and copies ran while one was open for 3% of the time, Pallas kernels for 0%

profile of v1, /device:TPU:1, one launch (start us, length us, event | category | flops | bytes accessed | tf_op | source)
XLA Modules:
  0.0 124.3 jit_solution(3375401121593872147)
XLA Ops:
  1.3 0.8 reshape.19.table_ref
  2.1 0.1 pad_add_fusion.place_ref
  2.2 0.0 copy-start
  2.2 2.8 %copy-done = bf16[32,7,7,2048]{3,0,2,1:T(8,128)(2,1)S(1)} copy-done((bf16[32,7,7,2048]{3,0,2,1:T(8,128)(2,1)S(1)}, bf16[32,7,7,2048]{3,0,2,1:T(8,128)(2,1)}, u32[]{:S(2)}) %copy-start) | copy-done | bytes 6422552
  5.0 0.0 copy-start.2
  5.0 1.6 %copy-done.2 = bf16[2048,512]{1,0:T(8,128)(2,1)S(1)} copy-done((bf16[2048,512]{1,0:T(8,128)(2,1)S(1)}, bf16[2048,512]{1,0:T(8,128)(2,1)}, u32[]{:S(2)}) %copy-start.2) | copy-done | bytes 2097176
  6.6 0.0 copy-start.5
  6.6 0.7 copy-done.5
  7.3 6.6 %reduce.1 = (bf16[1568,512]{1,0:T(8,128)(2,1)S(1)}, bf16[32,512]{1,0:T(8,128)(2,1)S(1)}, bf16[32,32]{1,0:T(8,128)(2,1)S(1)}, bf16[32,64,512]{2,1,0:T(8,128)(2,1)S(1)}) custom-call(s32[4]{0:T(128)S(1)} %pad_add_fusion.place_ref, bf16[1568,2048]{1,0:T(8,128)(2,1)S(1)} %bitcast.14, bf16[2048,512]{1,0:T(8,128)(2,1)S(1)} %copy-done.2, ...), custom_call_target="tpu_custom_call" | custom-call | tf_op jit(solution)/shard_map/reduce/pallas_call | solution.py:318
  13.9 0.0 copy-start.1
  13.9 36.3 %all_to_all.15.received_ref = bf16[32,64,512]{2,1,0:T(8,128)(2,1)S(1)} all-to-all(bf16[32,64,512]{2,1,0:T(8,128)(2,1)S(1)} %get-tuple-element.11), channel_id=1, replica_groups=mesh['group'=4,'member'=32] {'member'}, dimensions={0} | all-to-all | bytes 4194304 | tf_op jit(solution)/shard_map/all_to_all | solution.py:414
  50.3 0.0 copy-done.1
  50.3 0.0 copy-start.4
  50.3 0.0 copy-start.6
  50.3 16.2 %block.1 = (bf16[32,16,512]{2,1,0:T(8,128)(2,1)S(1)}, bf16[1024,128]{1,0:T(8,128)(2,1)S(1)}) custom-call(bf16[32,64,512]{2,1,0:T(8,128)(2,1)S(1)} %all_to_all.15.received_ref, bf16[3,1536,512]{2,1,0:T(8,128)(2,1)} %bitcast.15, bf16[512,2048]{1,0:T(8,128)(2,1)S(1)} %copy-done.1), custom_call_target="tpu_custom_call" | custom-call | tf_op jit(solution)/shard_map/block/pallas_call | solution.py:347
  66.5 14.9 %all_to_all.16.received_ref = bf16[32,16,512]{2,1,0:T(8,128)(2,1)S(1)} all-to-all(bf16[32,16,512]{2,1,0:T(8,128)(2,1)S(1)} %get-tuple-element.13), channel_id=1, replica_groups=mesh['group'=4,'member'=32] {'member'}, dimensions={0} | all-to-all | bytes 1048576 | tf_op jit(solution)/shard_map/all_to_all | solution.py:416
  81.4 0.0 copy-done.4
  81.4 0.0 copy-done.6
  81.4 0.0 copy-start.3
  81.4 15.8 %home.1 = (bf16[64,32,128]{2,1,0:T(8,128)(2,1)S(1)}, f32[1,32]{1,0:T(1,128)}) custom-call(bf16[32,16,512]{2,1,0:T(8,128)(2,1)S(1)} %all_to_all.16.received_ref, bf16[32,32]{1,0:T(8,128)(2,1)S(1)} %get-tuple-element.14.select_ref, bf16[1568,512]{1,0:T(8,128)(2,1)S(1)} %get-tuple-element.15.delta_ref, bf16[32,512]{1,0:T(8,128)(2,1)S(1)} %get-tuple-element.16.mean_ref, ...), custom_call_target="tpu_custom_call" | custom-call | tf_op jit(solution)/shard_map/home/pallas_call | solution.py:366
  97.2 17.9 %all_to_all.17.near_ref = bf16[64,32,128]{2,1,0:T(8,128)(2,1)S(1)} all-to-all(bf16[64,32,128]{2,1,0:T(8,128)(2,1)S(1)} %get-tuple-element.18), channel_id=1, replica_groups={{0,1,2,3,4,5,6,7,8,9,10,11,12,13,14,15,16,17,18,19,20,21,22,23,24,25,26..., dimensions={0} | all-to-all | bytes 1048576 | tf_op jit(solution)/shard_map/all_to_all | solution.py:422
  115.1 3.7 %collective-permute-start = (bf16[64,32,128]{2,1,0:T(8,128)(2,1)S(1)}, bf16[64,32,128]{2,1,0:T(8,128)(2,1)S(1)}, u32[]{:S(2)}, u32[]{:S(2)}) collective-permute-start(bf16[64,32,128]{2,1,0:T(8,128)(2,1)S(1)} %all_to_all.17.near_ref), channel_id=1, source_target_pairs={{0,32},{32,0},{64,96},{96,64},{1,33},{33,1},{65,97},{97,65},{2,34}... | collective-permute-start | bytes 1572872 | tf_op jit(solution)/shard_map/ppermute | solution.py:425
  118.9 0.0 copy-done.3
  118.9 3.3 %multiply_convert_fusion = bf16[1024,2048]{1,0:T(8,128)(2,1)} fusion(bf16[1024,128]{1,0:T(8,128)(2,1)S(1)} %get-tuple-element.12, bf16[2048,128]{1,0:T(8,128)(2,1)S(1)} %copy-done.3), kind=kOutput, calls=%fused_computation | convolution fusion | flops 541065216 | bytes 4980736 | tf_op jit(solution)/shard_map/dot_general | solution.py:39
  122.2 0.0 collective-permute-done.far_ref
  122.2 2.1 %queue.1 = bf16[2048,128]{1,0:T(8,128)(2,1)} custom-call(s32[4]{0:T(128)S(1)} %pad_add_fusion.place_ref, bf16[64,32,128]{2,1,0:T(8,128)(2,1)S(1)} %all_to_all.17.near_ref, bf16[64,32,128]{2,1,0:T(8,128)(2,1)S(1)} %collective-permute-done.far_ref, bf16[2048,128]{1,0:T(8,128)(2,1)S(1)} %copy-done.3), custom_call_target="tpu_custom_call" | custom-call | tf_op jit(solution)/shard_map/queue/pallas_call | solution.py:386
Async XLA Ops:
  2.2 2.8 %copy-start = (bf16[32,7,7,2048]{3,0,2,1:T(8,128)(2,1)S(1)}, bf16[32,7,7,2048]{3,0,2,1:T(8,128)(2,1)}, u32[]{:S(2)}) copy-start(bf16[32,7,7,2048]{3,0,2,1:T(8,128)(2,1)} %param.9) | copy-start | bytes 19267588
  5.0 1.6 %copy-start.2 = (bf16[2048,512]{1,0:T(8,128)(2,1)S(1)}, bf16[2048,512]{1,0:T(8,128)(2,1)}, u32[]{:S(2)}) copy-start(bf16[2048,512]{1,0:T(8,128)(2,1)} %weight_ref.1) | copy-start | bytes 6291460
  6.6 0.7 copy-start.5
  13.9 36.3 %copy-start.1 = (bf16[512,2048]{1,0:T(8,128)(2,1)S(1)}, bf16[512,2048]{1,0:T(8,128)(2,1)}, u32[]{:S(2)}) copy-start(bf16[512,2048]{1,0:T(8,128)(2,1)} %expand_hbm.3) | copy-start | bytes 6291460
  50.3 31.1 %copy-start.4 = (bf16[2048,128]{1,0:T(8,128)(2,1)S(1)}, bf16[2048,128]{1,0:T(8,128)(2,1)}, u32[]{:S(2)}) copy-start(bf16[2048,128]{1,0:T(8,128)(2,1)} %head_ref.1) | copy-start | bytes 1572868
  50.3 31.1 %copy-start.6 = (bf16[32,128]{1,0:T(8,128)(2,1)S(1)}, bf16[32,128]{1,0:T(8,128)(2,1)}, u32[]{:S(2)}) copy-start(bf16[32,128]{1,0:T(8,128)(2,1)} %query_ref.3) | copy-start | bytes 24580
  81.4 37.5 %copy-start.3 = (bf16[2048,128]{1,0:T(8,128)(2,1)S(1)}, bf16[2048,128]{1,0:T(8,128)(2,1)}, u32[]{:S(2)}) copy-start(bf16[2048,128]{1,0:T(8,128)(2,1)} %memory_ref.1) | copy-start | bytes 1572868
  115.1 7.0 %collective-permute-start = (bf16[64,32,128]{2,1,0:T(8,128)(2,1)S(1)}, bf16[64,32,128]{2,1,0:T(8,128)(2,1)S(1)}, u32[]{:S(2)}, u32[]{:S(2)}) collective-permute-start(bf16[64,32,128]{2,1,0:T(8,128)(2,1)S(1)} %all_to_all.17.near_ref), channel_id=1, source_target_pairs={{0,32},{32,0},{64,96},{96,64},{1,33},{33,1},{65,97},{97,65},{2,34}... | collective-permute-start | bytes 1572872 | tf_op jit(solution)/shard_map/ppermute | solution.py:425

commit v2 on v1

v2 whole, which is shorter than its diff:
```python
import jax
import jax.numpy as jnp
from jax import lax
from jax.experimental import pallas as pl
from jax.experimental.pallas import tpu as pltpu
from jax.sharding import PartitionSpec as P

norm_eps = 1e-05
unit_eps = 1e-06
sharpness_divisor = 0.2

IMAGES = 32
SIDE = 7
POSITIONS = SIDE * SIDE
ROW = SIDE * IMAGES
ROWS = POSITIONS * IMAGES
MID = 512
OUT = 2048
KEY = 128
SLAB = 8
SLABS = POSITIONS // SLAB
SIZE = SLAB * IMAGES
LAST = SLABS * MID
QUERIES = LAST + KEY
MESSAGE = QUERIES + MID
MOMENTS = 6 * KEY
MIB = 1 << 20
f32 = jnp.float32
bf16 = jnp.bfloat16


def iota(shape, dim):
    return lax.broadcasted_iota(jnp.int32, shape, dim)


def dot(a, b):
    return jnp.dot(a, b, preferred_element_type=f32)


def dot_tn(a, b):
    return lax.dot_general(a, b, (((0,), (0,)), ((), ())), preferred_element_type=f32)


def dot_nt(a, b):
    return lax.dot_general(a, b, (((1,), (1,)), ((), ())), preferred_element_type=f32)


def spread_select(select):
    left = (iota((SIZE, IMAGES), 0) // SLAB == iota((SIZE, IMAGES), 1)).astype(bf16)
    right = (iota((IMAGES, SIZE), 0) == iota((IMAGES, SIZE), 1) % IMAGES).astype(bf16)
    spread = dot(dot(left, select).astype(bf16), right)
    same = iota((SIZE, SIZE), 0) % SLAB == iota((SIZE, SIZE), 1) // IMAGES
    return jnp.where(same, spread, 0.0).astype(bf16)


def quarters(value):
    return jnp.concatenate([value[:, k * KEY : (k + 1) * KEY] for k in range(4)], axis=0)


def whole(pieces):
    return jnp.concatenate([pieces[k] for k in range(4)], axis=1)


def split(value):
    high = value.astype(bf16).astype(f32)
    return high, value - high


def unit_of(queries):
    query_f = queries.astype(f32)
    return query_f * lax.rsqrt(jnp.sum(query_f * query_f, axis=1, keepdims=True) + unit_eps)


def start_all(pairs, sems):
    copies = [pltpu.make_async_copy(a, b, sems.at[k]) for k, (a, b) in enumerate(pairs)]
    for copy in copies:
        copy.start()
    return copies


def peer_selector(place_ref, table):
    per_row = KEY // IMAGES
    block_rows = table[pl.ds(pl.multiple_of(place_ref[0] * SLAB, SLAB), SLAB), :]
    local = block_rows - (place_ref[0] * (IMAGES * IMAGES) + place_ref[1] * IMAGES)
    mine = jnp.logical_and(local >= 0, local < IMAGES)
    found = jnp.where(mine, local, 0).astype(f32).astype(bf16)
    by_block = (iota((IMAGES, SLAB), 0) // per_row == iota((IMAGES, SLAB), 1)).astype(bf16)
    inside = iota((IMAGES, KEY), 1) // IMAGES == iota((IMAGES, KEY), 0) % per_row
    chosen = jnp.sum(jnp.where(inside, dot(by_block, found), 0.0), axis=1, keepdims=True)
    return (chosen == iota((IMAGES, IMAGES), 1).astype(f32)).astype(bf16)


def reduce_kernel(
    place_ref, x_hbm, weight_hbm, table_hbm, query_hbm, spatial_hbm, expand_hbm,
    x, spatial_weight, expand_weight, delta, mean_ref, select_ref, message,
    weight, table, query, sems,
):
    map_rows = [pl.ds(y * ROW, ROW) for y in range(SIDE)]
    weight_rows = [pl.ds(k * MID, MID) for k in range(OUT // MID)]
    loads = start_all(
        [(table_hbm, table), (query_hbm, query)]
        + [(weight_hbm.at[rows, :], weight.at[rows, :]) for rows in weight_rows]
        + [(x_hbm.at[rows, :], x.at[rows, :]) for rows in map_rows]
        + [(spatial_hbm.at[k], spatial_weight.at[k]) for k in range(3)]
        + [(expand_hbm, expand_weight)],
        sems,
    )

    loads[0].wait()
    loads[1].wait()
    select = peer_selector(place_ref, table)
    select_ref[...] = select
    mover = spread_select(select)
    unit = unit_of(query[...])
    unit = jnp.concatenate([unit[SLAB * k : SLAB * (k + 1)] for k in range(4)], axis=1)
    message[:, :, pl.ds(QUERIES, MID)] = jnp.broadcast_to(unit[None], (IMAGES, SLAB, MID)).astype(bf16)
    for copy in loads[2:6]:
        copy.wait()
    done = [0]
    parts = []

    def finish(y):
        delta[map_rows[y], :] = (parts[y] - mean_f[None]).reshape(ROW, MID).astype(bf16)
        while (done[0] + 1) * SLAB <= (y + 1) * SIDE:
            moved = dot(mover, delta[pl.ds(done[0] * SIZE, SIZE), :]).reshape(IMAGES, SLAB, MID)
            message[:, :, pl.ds(done[0] * MID, MID)] = moved.astype(bf16)
            done[0] += 1

    for y in range(SIDE):
        for k in {0: [0], 1: [1, 2, 3], 4: [4, 5, 6]}.get(y, ()):
            loads[6 + k].wait()
        part = dot(x[map_rows[y], :], weight[...]).reshape(SIDE, IMAGES, MID)
        if y == 0:
            mean = (jnp.sum(part, axis=0) * (1.0 / SIDE)).astype(bf16)
            mean_f = mean.astype(f32)
            mean_ref[...] = mean
        if y > 0:
            finish(y - 1)
        parts.append(part)
    finish(SIDE - 1)
    last = jnp.concatenate([quarters(delta[pl.ds(SLABS * SIZE, IMAGES), :]), quarters(mean)], axis=0)
    message[:, :, pl.ds(LAST, KEY)] = dot(mover, last).reshape(IMAGES, SLAB, KEY).astype(bf16)
    for copy in loads[6 + SIDE :]:
        copy.wait()


def store_windows(windows, reduced, y):
    edge = jnp.zeros((IMAGES, MID), bf16)
    at = (y + 1) * ROW
    windows[pl.ds(at, IMAGES), pl.ds(0, MID)] = edge
    windows[pl.ds(at + IMAGES, ROW - IMAGES), pl.ds(0, MID)] = reduced[: ROW - IMAGES]
    windows[pl.ds(at, ROW), pl.ds(MID, MID)] = reduced
    windows[pl.ds(at, ROW - IMAGES), pl.ds(2 * MID, MID)] = reduced[IMAGES:]
    windows[pl.ds(at + ROW - IMAGES, IMAGES), pl.ds(2 * MID, MID)] = edge


def clear_border(windows):
    border = jnp.zeros((ROW, 3 * MID), bf16)
    windows[pl.ds(0, ROW), :] = border
    windows[pl.ds((SIDE + 1) * ROW, ROW), :] = border


def convolve_row(windows, spatial_weight, y):
    return (
        dot(windows[pl.ds(y * ROW, ROW), :], spatial_weight[0])
        + dot(windows[pl.ds((y + 1) * ROW, ROW), :], spatial_weight[1])
        + dot(windows[pl.ds((y + 2) * ROW, ROW), :], spatial_weight[2])
    )


def fold(value):
    return jnp.sum(value.reshape(-1, IMAGES, value.shape[1]), axis=0)


def block_mean(total):
    return jnp.sum(total, axis=0, keepdims=True) * (1.0 / ROWS)


def block_kernel(received, spatial_weight, expand_weight, moments, units, values, windows, spatial):
    clear_border(windows)
    row, column = iota((SIZE, SIZE), 0), iota((SIZE, SIZE), 1)
    mover = jnp.logical_and(row % IMAGES == column // SLAB, row // IMAGES == column % SLAB).astype(bf16)

    tail = dot(mover, received[:, :, pl.ds(LAST, KEY)].reshape(SIZE, KEY)).reshape(SLAB, IMAGES, KEY)
    mean = whole(tail[4:])
    shift = jnp.sum(mean, axis=0, keepdims=True) * (1.0 / IMAGES)
    away = mean - shift
    last = whole(tail[:4]) + away
    values[pl.ds(SLABS * SIZE, IMAGES), :] = last
    total, squares = last, last * last
    for slab in range(SLABS):
        moved = dot(mover, received[:, :, pl.ds(slab * MID, MID)].reshape(SIZE, MID))
        moved = (moved.reshape(SLAB, IMAGES, MID) + away[None]).reshape(SIZE, MID)
        values[pl.ds(slab * SIZE, SIZE), :] = moved
        total = total + fold(moved)
        squares = squares + fold(moved * moved)
    offset1 = block_mean(total)
    center1 = shift + offset1
    scale1 = lax.rsqrt(block_mean(squares) - offset1 * offset1 + norm_eps).astype(bf16).astype(f32)
    for y in range(SIDE):
        reduced = jnp.maximum((values[pl.ds(y * ROW, ROW), :] - offset1) * scale1, 0.0)
        store_windows(windows, reduced.astype(bf16), y)

    queries = received[:, :, pl.ds(QUERIES, MID)].astype(f32)
    queries = jnp.concatenate([queries[:, None, :, k * KEY : (k + 1) * KEY] for k in range(4)], axis=1)
    units[...] = queries.reshape(IMAGES * IMAGES, KEY).astype(bf16)

    total = squares = jnp.zeros((IMAGES, MID), f32)
    for y in range(SIDE):
        second = convolve_row(windows, spatial_weight, y)
        values[pl.ds(y * ROW, ROW), :] = second
        total = total + fold(second)
        squares = squares + fold(second * second)
    center2 = block_mean(total)
    scale2 = lax.rsqrt(block_mean(squares) - center2 * center2 + norm_eps).astype(bf16).astype(f32)
    total = jnp.zeros((IMAGES, MID), f32)
    for y in range(SIDE):
        rows = pl.ds(y * ROW, ROW)
        kept = jnp.maximum((values[rows, :] - center2) * scale2, 0.0).astype(bf16)
        spatial[rows, :] = kept
        total = total + fold(kept.astype(f32))
    mean_high, mean_low = split(block_mean(total))

    scale3 = []
    for part in range(OUT // MID):
        weight = expand_weight[:, pl.ds(part * MID, MID)]
        center3 = dot(mean_high.astype(bf16), weight) + dot(mean_low.astype(bf16), weight)
        squares = jnp.zeros((IMAGES, MID), f32)
        for y in range(SIDE):
            third = dot(spatial[pl.ds(y * ROW, ROW), :], weight)
            squares = squares + fold(third * third)
        scale3.append(lax.rsqrt(block_mean(squares) - center3 * center3 + norm_eps))

    vectors = [*split(center1), *split(center2), mean_high, mean_low, scale1, scale2, *scale3]
    vectors = [quarters(vector) for vector in vectors]
    tiles = [jnp.concatenate(vectors[k : k + 2], axis=0) for k in range(0, 12, 2)]
    packed = jnp.concatenate(tiles, axis=1)
    moments[...] = jnp.broadcast_to(packed[None], (IMAGES, SLAB, MOMENTS)).astype(bf16)


def home_kernel(
    received, select, mean, delta, spatial_weight, expand_weight, x, head, query,
    keys, similarity_ref, windows, spatial, pooled,
):
    clear_border(windows)
    stats = dot_tn(spread_select(select[...]), received[...].reshape(SIZE, MOMENTS))
    stats = stats.reshape(SLAB, IMAGES, MOMENTS)
    vectors = []
    for k in range(12):
        half, lanes = 4 * (k % 2), k // 2 * KEY
        vectors.append(whole([stats[half + q, :, lanes : lanes + KEY] for q in range(4)]))
    offset1 = mean[...].astype(f32) - (vectors[0] + vectors[1])
    center2 = vectors[2] + vectors[3]
    mean_high, mean_low = vectors[4].astype(bf16), vectors[5].astype(bf16)
    scale1, scale2 = vectors[6], vectors[7]

    for y in range(SIDE):
        away = delta[pl.ds(y * ROW, ROW), :].astype(f32).reshape(SIDE, IMAGES, MID)
        reduced = jnp.maximum((away + offset1[None]) * scale1[None], 0.0)
        store_windows(windows, reduced.reshape(ROW, MID).astype(bf16), y)

    for y in range(SIDE):
        second = convolve_row(windows, spatial_weight, y).reshape(SIDE, IMAGES, MID)
        kept = jnp.maximum((second - center2[None]) * scale2[None], 0.0)
        spatial[pl.ds(y * ROW, ROW), :] = kept.reshape(ROW, MID).astype(bf16)

    for part in range(OUT // MID):
        columns = pl.ds(part * MID, MID)
        weight = expand_weight[:, columns]
        center3 = dot(mean_high, weight) + dot(mean_low, weight)
        scale3 = vectors[8 + part]
        total = jnp.zeros((IMAGES, MID), f32)
        for y in range(SIDE):
            rows = pl.ds(y * ROW, ROW)
            third = dot(spatial[rows, :], weight).reshape(SIDE, IMAGES, MID)
            kept = x[rows, columns].astype(f32).reshape(SIDE, IMAGES, MID)
            merged = jnp.maximum((third - center3[None]) * scale3[None] + kept, 0.0)
            total = total + jnp.sum(merged, axis=0)
        pooled[:, columns] = (total * (1.0 / POSITIONS)).astype(bf16)
    projected = dot(pooled[...], head[...])
    key = projected * lax.rsqrt(jnp.sum(projected * projected, axis=1, keepdims=True) + unit_eps)
    key = key.astype(bf16)
    keys[...] = jnp.broadcast_to(key[None], keys.shape)
    unit = unit_of(query[...]).astype(bf16)
    pairs = dot_nt(unit, key)
    own = iota((IMAGES, IMAGES), 0) == iota((IMAGES, IMAGES), 1)
    similarity_ref[...] = jnp.sum(jnp.where(own, pairs, 0.0), axis=0, keepdims=True) / sharpness_divisor


def logits_kernel(units_ref, memory_ref, out_ref):
    out_ref[...] = (dot_nt(units_ref[...], memory_ref[...]) * (1.0 / sharpness_divisor)).astype(bf16)


def queue_kernel(place_ref, near_hbm, far_hbm, memory_hbm, out_ref, padded, memory, sems):
    slots = memory.shape[0]
    batch = 4 * IMAGES * IMAGES
    half = IMAGES * IMAGES
    core = place_ref[2]
    start = place_ref[3]
    pairs = [(memory_hbm, memory)]
    for high in range(2):
        for ref, which in ((near_hbm, core), (far_hbm, 1 - core)):
            at = pl.multiple_of(slots + (2 * high + which) * half, half)
            pairs.append((ref.at[pl.ds(high * half, half), :], padded.at[pl.ds(at, half), :]))
    loads = start_all(pairs, sems)
    edge = jnp.zeros((slots, KEY), bf16)
    padded[pl.ds(0, slots), :] = edge
    padded[pl.ds(slots + batch, slots), :] = edge
    padded[pl.ds(2 * slots + batch, ALIGN), :] = edge[:ALIGN]
    base = start // ALIGN * ALIGN
    inner = start - base
    pick = (iota((TILE, TILE + ALIGN), 1) == iota((TILE, TILE + ALIGN), 0) + inner).astype(bf16)
    for copy in loads:
        copy.wait()
    for part in range(slots // TILE):
        rows = padded[pl.ds(pl.multiple_of(base + part * TILE, ALIGN), TILE + ALIGN), :]
        fresh = dot(pick, rows)
        index = start - slots + part * TILE + iota((TILE, KEY), 0)
        inside = jnp.logical_and(index >= 0, index < batch)
        old = memory[pl.ds(part * TILE, TILE), :].astype(f32)
        out_ref[pl.ds(part * TILE, TILE), :] = jnp.where(inside, fresh, old).astype(bf16)


ALIGN = 16
TILE = 256


def params(mib):
    return pltpu.CompilerParams(vmem_limit_bytes=mib * MIB)


VMEM = pl.BlockSpec(memory_space=pltpu.VMEM)
SMEM = pl.BlockSpec(memory_space=pltpu.SMEM)
ANY = pl.BlockSpec(memory_space=pl.ANY)
HBM = pl.BlockSpec(memory_space=pltpu.HBM)


def shape(*dims, dtype=bf16):
    return jax.ShapeDtypeStruct(dims, dtype)


def scratch(*dims, dtype=bf16):
    return pltpu.VMEM(dims, dtype)


def dma(count):
    return pltpu.SemaphoreType.DMA((count,))


def in_hbm(*arrays):
    return [pltpu.with_memory_space_constraint(array, pltpu.HBM) for array in arrays]


def in_vmem(*arrays):
    return [pltpu.with_memory_space_constraint(array, pltpu.VMEM) for array in arrays]


def reduce_call(place, x, conv_reduce, table, queries, conv_spatial, conv_expand):
    return pl.pallas_call(
        reduce_kernel,
        in_specs=[SMEM] + [HBM] * 6,
        out_specs=[VMEM] * 7,
        out_shape=[
            scratch(ROWS, OUT),
            scratch(*conv_spatial.shape),
            scratch(MID, OUT),
            scratch(ROWS, MID),
            scratch(IMAGES, MID),
            scratch(IMAGES, IMAGES),
            scratch(IMAGES, SLAB, MESSAGE),
        ],
        scratch_shapes=[
            scratch(OUT, MID),
            scratch(*table.shape, dtype=jnp.int32),
            scratch(IMAGES, KEY),
            dma(10 + SIDE),
        ],
        compiler_params=params(24),
        name="reduce",
    )(place, *in_hbm(x, conv_reduce, table, queries, conv_spatial, conv_expand))


def block_call(received, spatial_weight, expand_weight):
    return pl.pallas_call(
        block_kernel,
        in_specs=[VMEM] * 3,
        out_specs=[VMEM, VMEM],
        out_shape=[scratch(IMAGES, SLAB, MOMENTS), scratch(IMAGES * IMAGES, KEY)],
        scratch_shapes=[
            scratch(ROWS, MID, dtype=f32),
            scratch(ROWS + 2 * ROW, 3 * MID),
            scratch(ROWS, MID),
        ],
        compiler_params=params(30),
        name="block",
    )(*in_vmem(received, spatial_weight, expand_weight))


def home_call(received, select, mean, delta, spatial_weight, expand_weight, x, key_head, queries, copies):
    return pl.pallas_call(
        home_kernel,
        in_specs=[VMEM] * 9,
        out_specs=[VMEM, VMEM],
        out_shape=[scratch(copies, IMAGES, KEY), shape(1, IMAGES, dtype=f32)],
        scratch_shapes=[
            scratch(ROWS + 2 * ROW, 3 * MID),
            scratch(ROWS, MID),
            scratch(IMAGES, OUT),
        ],
        compiler_params=params(30),
        name="home",
    )(*in_vmem(received, select, mean, delta, spatial_weight, expand_weight, x), key_head, queries)


def logits_call(units, memory):
    rows, columns = units.shape[0], memory.shape[0]
    step = 128
    return pl.pallas_call(
        logits_kernel,
        grid=(rows // step,),
        in_specs=[
            pl.BlockSpec((step, KEY), lambda at: (at, 0)),
            pl.BlockSpec((columns, KEY), lambda at: (0, 0)),
        ],
        out_specs=pl.BlockSpec((step, columns), lambda at: (at, 0)),
        out_shape=shape(rows, columns),
        compiler_params=params(12),
        cost_estimate=pl.CostEstimate(
            flops=2 * rows * columns * KEY, bytes_accessed=2 * rows * columns, transcendentals=0
        ),
        name="logits",
    )(units, memory)


def queue_call(place, near, far, memory):
    return pl.pallas_call(
        queue_kernel,
        in_specs=[SMEM, ANY, ANY, ANY],
        out_specs=VMEM,
        out_shape=shape(*memory.shape),
        scratch_shapes=[
            scratch(2 * memory.shape[0] + 4 * IMAGES * IMAGES + ALIGN, KEY),
            scratch(*memory.shape),
            dma(5),
        ],
        compiler_params=params(32),
        name="queue",
    )(place, near.reshape(-1, KEY), far.reshape(-1, KEY), memory)


def per_device(
    activations, shuffle, pointer, conv_reduce, conv_spatial, conv_expand, key_head, queries, negative_memory
):
    group, member = lax.axis_index("group"), lax.axis_index("member")
    members = lax.axis_size("member")
    slots = negative_memory.shape[0]
    total_slots = slots * members
    batch = shuffle.shape[0]
    offset = jnp.mod(member * slots - pointer[0], total_slots)
    wrapped = jnp.where(offset > total_slots - slots, offset - total_slots, batch)
    start = slots + jnp.where(offset < batch, offset, wrapped)
    place = jnp.stack([group, member, group % 2, start]).astype(jnp.int32)

    x = activations.transpose(1, 2, 0, 3).reshape(ROWS, OUT)
    spatial_weight = conv_spatial.reshape(3, 3 * MID, MID)
    table = shuffle.reshape(batch // KEY, KEY)
    x, spatial_weight, expand_weight, delta, mean, select, message = reduce_call(
        place, x, conv_reduce, table, queries, spatial_weight, conv_expand
    )
    received = lax.all_to_all(message, "member", split_axis=0, concat_axis=0, tiled=True)
    moments, units = block_call(received, spatial_weight, expand_weight)
    returned = lax.all_to_all(moments, "member", split_axis=0, concat_axis=0, tiled=True)
    copies, similarity = home_call(
        returned, select, mean, delta, spatial_weight, expand_weight, x, key_head, queries, 2 * members
    )
    copies, units = lax.optimization_barrier((copies, units))
    logits = logits_call(units, negative_memory)
    same_core = [[g * members + m for g in (core, core + 2) for m in range(members)] for core in (0, 1)]
    near = lax.all_to_all(
        copies, ("group", "member"), split_axis=0, concat_axis=0, tiled=True, axis_index_groups=same_core
    )
    near, logits = lax.optimization_barrier((near, logits))
    far = lax.ppermute(near, "group", [(0, 1), (1, 0), (2, 3), (3, 2)])
    new_queue = queue_call(place, near, far, negative_memory)
    return logits, similarity.reshape(IMAGES), new_queue


def solution(mesh):
    placed = (
        P(("group", "member"), None, None, None),
        P(),
        P(),
        P(),
        P(),
        P(),
        P(),
        P(("group", "member"), None),
        P("member", None),
    )
    return jax.shard_map(
        per_device,
        mesh=mesh,
        in_specs=placed,
        out_specs=(P("group", "member"), P(("group", "member")), P("member", None)),
        check_vma=False,
    )
```

time: 125 us -> 110 us (0.88)
  blocking collectives: 69.1 us -> 48.3 us
  waiting for transfers between devices: 0.01 us -> 7.64 us
  starting transfers between devices: 3.74 us -> 10.2 us
  local copies, waits for them, and re-layouts: 5.92 us -> 0.01 us
  matrix products: 3.27 us -> 0 us
    all_to_all x1 -> x0, blocking collectives: 17.9 us -> none  [per_device(): lax.all_to_all(copies, ('group', 'member'), split_axis=0, concat_axis=0,...]
    all_to_all x0 -> x1, starting transfers between devices: none -> 6.52 us  [per_device(): lax.all_to_all(copies, ('group', 'member'), split_axis=0, concat_axis=0,...]
    all_to_all x0 -> x1, waiting for transfers between devices: none -> 6.11 us  [per_device(): lax.all_to_all(copies, ('group', 'member'), split_axis=0, concat_axis=0,...]
    unnamed x14 -> x6, local copies, waits for them, and re-layouts: 5.13 us -> 0.01 us
    dot_general x1 -> x0, matrix products: 3.27 us -> none  [dot_nt(): lax.dot_general(a, b, (((1,), (1,)), ((), ())), preferred_element_type=f32)]
    all_to_all x1, blocking collectives: 36.3 us -> 34.1 us  [per_device(): lax.all_to_all(message, 'member', split_axis=0, concat_axis=0, tiled=True)]
    ppermute x1, waiting for transfers between devices: 0.01 us -> 1.54 us  [per_device(): far = lax.ppermute(near, 'group', [(0, 1), (1, 0), (2, 3), (3, 2)])]
    pallas_call x4 -> x5, Pallas kernels: 40.8 us -> 41.6 us  [the longest x1 14.1 us: home_call(): pl.pallas_call(home_kernel, in_specs=[VMEM] * 9, out_specs=[VMEM, VMEM],...]
  transfers between devices with their start and end apart: 1 -> 2, of which waited for: 0 -> 2; matrix products, arithmetic and copies ran while one was open for 3% -> 0% of each run, Pallas kernels for 0% -> 4%
where the time goes in v2:
time: 110 us; the launch traced here: 109 us
  blocking collectives  48.3 us (44%)
  Pallas kernels  41.6 us (38%)
  starting transfers between devices  10.2 us (9%)
  waiting for transfers between devices  7.64 us (7%)
  between operations  1.53 us (1%)
    all_to_all x1, blocking collectives, per_device(): lax.all_to_all(message, 'member', split_axis=0, concat_axis=0, tiled=True)  34.1 us
    all_to_all x1, blocking collectives, per_device(): lax.all_to_all(moments, 'member', split_axis=0, concat_axis=0, tiled=True)  14.2 us
    pallas_call x1, Pallas kernels, home_call(): pl.pallas_call(home_kernel, in_specs=[VMEM] * 9, out_specs=[VMEM, VMEM],...  14.1 us
    pallas_call x1, Pallas kernels, block_call(): pl.pallas_call(block_kernel, in_specs=[VMEM] * 3, out_specs=[VMEM, VMEM],...  13.5 us
    pallas_call x1, Pallas kernels, reduce_call(): pl.pallas_call(reduce_kernel, in_specs=[SMEM] + [HBM] * 6, out_specs=[VME...  7.1 us
    all_to_all x1, starting transfers between devices, per_device(): lax.all_to_all(copies, ('group', 'member'), split_axis=0, concat_axis=0,...  6.52 us
    all_to_all x1, waiting for transfers between devices, per_device(): lax.all_to_all(copies, ('group', 'member'), split_axis=0, concat_axis=0,...  6.11 us
    pallas_call x1, Pallas kernels, logits_call(): pl.pallas_call(logits_kernel, grid=(rows // step,), in_specs=[pl.BlockSpe...  4.7 us
  transfers between devices with their start and end apart: 2, of which 2 were waited for; matrix products, arithmetic and copies ran while one was open for 0% of the time, Pallas kernels for 4%

profile of v2, /device:TPU:1, one launch (start us, length us, event | category | flops | bytes accessed | tf_op | source)
XLA Modules:
  0.0 109.4 jit_solution(773776651698607755)
XLA Ops:
  1.3 0.1 pad_add_fusion.place_ref
  1.4 7.1 %reduce.1 = (bf16[1568,2048]{1,0:T(8,128)(2,1)S(1)}, bf16[3,1536,512]{2,1,0:T(8,128)(2,1)S(1)}, bf16[512,2048]{1,0:T(8,128)(2,1)S(1)}, bf16[1568,512]{1,0:T(8,12...) custom-call(s32[4]{0:T(128)S(1)} %pad_add_fusion.place_ref, ...), custom_call_target="tpu_custom_call" | custom-call | tf_op jit(solution)/shard_map/reduce/pallas_call | solution.py:359
  8.5 34.1 %all_to_all.15.received = bf16[32,8,3712]{2,1,0:T(8,128)(2,1)S(1)} all-to-all(bf16[32,8,3712]{2,1,0:T(8,128)(2,1)S(1)} %get-tuple-element.18), channel_id=1, replica_groups=mesh['group'=4,'member'=32] {'member'}, dimensions={0} | all-to-all | bytes 3801088 | tf_op jit(solution)/shard_map/all_to_all | solution.py:470
  42.6 0.0 copy-start.1
  42.6 0.0 copy-start.2
  42.6 13.5 %block.1 = (bf16[32,8,768]{2,1,0:T(8,128)(2,1)S(1)}, bf16[1024,128]{1,0:T(8,128)(2,1)S(1)}) custom-call(bf16[32,8,3712]{2,1,0:T(8,128)(2,1)S(1)} %all_to_all.15.received, bf16[3,1536,512]{2,1,0:T(8,128)(2,1)S(1)} %get-tuple-element.19.spatial_weight, bf16[512,2048]{1,0:T(8,128)(2,1)S(1)} %get-tuple-element.20.expand_weight), custom_call_target="tpu_custom_call" | custom-call | tf_op jit(solution)/shard_map/block/pallas_call | solution.py:384
  56.1 14.2 %all_to_all.16.received = bf16[32,8,768]{2,1,0:T(8,128)(2,1)S(1)} all-to-all(bf16[32,8,768]{2,1,0:T(8,128)(2,1)S(1)} %get-tuple-element.21), channel_id=1, replica_groups=mesh['group'=4,'member'=32] {'member'}, dimensions={0} | all-to-all | bytes 786432 | tf_op jit(solution)/shard_map/all_to_all | solution.py:472
  70.3 0.0 copy-done.1
  70.3 0.0 copy-done.2
  70.3 0.0 copy-start
  70.3 14.1 %home.1 = (bf16[64,32,128]{2,1,0:T(8,128)(2,1)}, f32[1,32]{1,0:T(1,128)}) custom-call(bf16[32,8,768]{2,1,0:T(8,128)(2,1)S(1)} %all_to_all.16.received, bf16[32,32]{1,0:T(8,128)(2,1)S(1)} %get-tuple-element.22.select, bf16[32,512]{1,0:T(8,128)(2,1)S(1)} %get-tuple-element.23.mean, bf16[1568,512]{1,0:T(8,128)(2,1)S(1)} %get-tuple-element.24.delta, ...), custom_call_target="tpu_custom_call" | custom-call | tf_op jit(solution)/shard_map/home/pallas_call | solution.py:400
  84.4 6.5 %all-to-all-start.2 = ((bf16[64,32,128]{2,1,0:T(8,128)(2,1)}), bf16[64,32,128]{2,1,0:T(8,128)(2,1)S(1)}, u32[]{:S(2)}, u32[]{:S(2)}) async-start(bf16[64,32,128]{2,1,0:T(8,128)(2,1)} %get-tuple-element.28), calls=%async_computation.2 | async-start | bytes 1048576 | tf_op jit(solution)/shard_map/all_to_all | solution.py:479
  90.9 0.0 copy-done
  90.9 4.7 %logits.1 = bf16[1024,2048]{1,0:T(8,128)(2,1)} custom-call(bf16[1024,128]{1,0:T(8,128)(2,1)S(1)} %get-tuple-element.29.units_ref, bf16[2048,128]{1,0:T(8,128)(2,1)S(1)} %copy-done), custom_call_target="tpu_custom_call" | custom-call | flops 536870912 | bytes 4194304 | tf_op jit(solution)/shard_map/logits/pallas_call | solution.py:418
  95.6 6.1 %all-to-all-done.2 = bf16[64,32,128]{2,1,0:T(8,128)(2,1)S(1)} async-done(((bf16[64,32,128]{2,1,0:T(8,128)(2,1)}), bf16[64,32,128]{2,1,0:T(8,128)(2,1)S(1)}, u32[]{:S(2)}, u32[]{:S(2)}) %all-to-all-start.2) | async-done | bytes 524320 | tf_op jit(solution)/shard_map/all_to_all | solution.py:479
  101.7 3.7 %collective-permute-start = (bf16[64,32,128]{2,1,0:T(8,128)(2,1)S(1)}, bf16[64,32,128]{2,1,0:T(8,128)(2,1)S(1)}, u32[]{:S(2)}, u32[]{:S(2)}) collective-permute-start(bf16[64,32,128]{2,1,0:T(8,128)(2,1)S(1)} %all-to-all-done.2), channel_id=1, source_target_pairs={{0,32},{32,0},{64,96},{96,64},{1,33},{33,1},{65,97},{97,65},{2,34}... | collective-permute-start | bytes 1572872 | tf_op jit(solution)/shard_map/ppermute | solution.py:483
  105.5 1.5 %collective-permute-done = bf16[64,32,128]{2,1,0:T(8,128)(2,1)S(1)} collective-permute-done((bf16[64,32,128]{2,1,0:T(8,128)(2,1)S(1)}, bf16[64,32,128]{2,1,0:T(8,128)(2,1)S(1)}, u32[]{:S(2)}, u32[]{:S(2)}) %collective-permute-start) | collective-permute-done | bytes 524320 | tf_op jit(solution)/shard_map/ppermute | solution.py:483
  107.0 2.2 %queue.1 = bf16[2048,128]{1,0:T(8,128)(2,1)} custom-call(s32[4]{0:T(128)S(1)} %pad_add_fusion.place_ref, bf16[2048,128]{1,0:T(8,128)(2,1)S(1)} %bitcast.14, bf16[2048,128]{1,0:T(8,128)(2,1)S(1)} %bitcast.15, bf16[2048,128]{1,0:T(8,128)(2,1)S(1)} %copy-done), custom_call_target="tpu_custom_call" | custom-call | tf_op jit(solution)/shard_map/queue/pallas_call | solution.py:436
Async XLA Ops:
  42.6 27.7 %copy-start.1 = (bf16[2048,128]{1,0:T(8,128)(2,1)S(1)}, bf16[2048,128]{1,0:T(8,128)(2,1)}, u32[]{:S(2)}) copy-start(bf16[2048,128]{1,0:T(8,128)(2,1)} %head.1) | copy-start | bytes 1572868
  42.6 27.7 %copy-start.2 = (bf16[32,128]{1,0:T(8,128)(2,1)S(1)}, bf16[32,128]{1,0:T(8,128)(2,1)}, u32[]{:S(2)}) copy-start(bf16[32,128]{1,0:T(8,128)(2,1)} %query.1) | copy-start | bytes 24580
  70.3 20.6 %copy-start = (bf16[2048,128]{1,0:T(8,128)(2,1)S(1)}, bf16[2048,128]{1,0:T(8,128)(2,1)}, u32[]{:S(2)}) copy-start(bf16[2048,128]{1,0:T(8,128)(2,1)} %memory_hbm.1) | copy-start | bytes 1572868
  84.4 17.4 %all-to-all-start.2 = ((bf16[64,32,128]{2,1,0:T(8,128)(2,1)}), bf16[64,32,128]{2,1,0:T(8,128)(2,1)S(1)}, u32[]{:S(2)}, u32[]{:S(2)}) async-start(bf16[64,32,128]{2,1,0:T(8,128)(2,1)} %get-tuple-element.28), calls=%async_computation.2 | async-start | bytes 1048576 | tf_op jit(solution)/shard_map/all_to_all | solution.py:479
  101.7 5.3 %collective-permute-start = (bf16[64,32,128]{2,1,0:T(8,128)(2,1)S(1)}, bf16[64,32,128]{2,1,0:T(8,128)(2,1)S(1)}, u32[]{:S(2)}, u32[]{:S(2)}) collective-permute-start(bf16[64,32,128]{2,1,0:T(8,128)(2,1)S(1)} %all-to-all-done.2), channel_id=1, source_target_pairs={{0,32},{32,0},{64,96},{96,64},{1,33},{33,1},{65,97},{97,65},{2,34}... | collective-permute-start | bytes 1572872 | tf_op jit(solution)/shard_map/ppermute | solution.py:483

commit v3 on v2

--- a/solution.py
+++ b/solution.py
@@ -161,10 +161,9 @@
 
 
 def convolve_row(windows, spatial_weight, y):
-    return (
-        dot(windows[pl.ds(y * ROW, ROW), :], spatial_weight[0])
-        + dot(windows[pl.ds((y + 1) * ROW, ROW), :], spatial_weight[1])
-        + dot(windows[pl.ds((y + 2) * ROW, ROW), :], spatial_weight[2])
+    return dot(
+        jnp.concatenate([windows[pl.ds((y + k) * ROW, ROW), :] for k in range(3)], axis=1),
+        spatial_weight[...].reshape(9 * MID, MID),
     )
 
 
@@ -176,7 +175,7 @@
     return jnp.sum(total, axis=0, keepdims=True) * (1.0 / ROWS)
 
 
-def block_kernel(received, spatial_weight, expand_weight, moments, units, values, windows, spatial):
+def block_kernel(received, spatial_weight, expand_weight, moments, units, values, windows, square_sums):
     clear_border(windows)
     row, column = iota((SIZE, SIZE), 0), iota((SIZE, SIZE), 1)
     mover = jnp.logical_and(row % IMAGES == column // SLAB, row // IMAGES == column % SLAB).astype(bf16)
@@ -197,16 +196,19 @@
     offset1 = block_mean(total)
     center1 = shift + offset1
     scale1 = lax.rsqrt(block_mean(squares) - offset1 * offset1 + norm_eps).astype(bf16).astype(f32)
-    for y in range(SIDE):
-        reduced = jnp.maximum((values[pl.ds(y * ROW, ROW), :] - offset1) * scale1, 0.0)
-        store_windows(windows, reduced.astype(bf16), y)
-
     queries = received[:, :, pl.ds(QUERIES, MID)].astype(f32)
     queries = jnp.concatenate([queries[:, None, :, k * KEY : (k + 1) * KEY] for k in range(4)], axis=1)
     units[...] = queries.reshape(IMAGES * IMAGES, KEY).astype(bf16)
 
+    def normalize(y):
+        reduced = jnp.maximum((values[pl.ds(y * ROW, ROW), :] - offset1) * scale1, 0.0)
+        store_windows(windows, reduced.astype(bf16), y)
+
+    normalize(0)
     total = squares = jnp.zeros((IMAGES, MID), f32)
     for y in range(SIDE):
+        if y + 1 < SIDE:
+            normalize(y + 1)
         second = convolve_row(windows, spatial_weight, y)
         values[pl.ds(y * ROW, ROW), :] = second
         total = total + fold(second)
@@ -214,22 +216,20 @@
     center2 = block_mean(total)
     scale2 = lax.rsqrt(block_mean(squares) - center2 * center2 + norm_eps).astype(bf16).astype(f32)
     total = jnp.zeros((IMAGES, MID), f32)
+    parts = range(OUT // MID)
     for y in range(SIDE):
-        rows = pl.ds(y * ROW, ROW)
-        kept = jnp.maximum((values[rows, :] - center2) * scale2, 0.0).astype(bf16)
-        spatial[rows, :] = kept
+        kept = jnp.maximum((values[pl.ds(y * ROW, ROW), :] - center2) * scale2, 0.0).astype(bf16)
         total = total + fold(kept.astype(f32))
+        for part in parts:
+            third = dot(kept, expand_weight[:, pl.ds(part * MID, MID)])
+            square = fold(third * third)
+            square_sums[part] = square if y == 0 else square_sums[part] + square
     mean_high, mean_low = split(block_mean(total))
-
     scale3 = []
-    for part in range(OUT // MID):
+    for part in parts:
         weight = expand_weight[:, pl.ds(part * MID, MID)]
         center3 = dot(mean_high.astype(bf16), weight) + dot(mean_low.astype(bf16), weight)
-        squares = jnp.zeros((IMAGES, MID), f32)
-        for y in range(SIDE):
-            third = dot(spatial[pl.ds(y * ROW, ROW), :], weight)
-            squares = squares + fold(third * third)
-        scale3.append(lax.rsqrt(block_mean(squares) - center3 * center3 + norm_eps))
+        scale3.append(lax.rsqrt(block_mean(square_sums[part]) - center3 * center3 + norm_eps))
 
     vectors = [*split(center1), *split(center2), mean_high, mean_low, scale1, scale2, *scale3]
     vectors = [quarters(vector) for vector in vectors]
@@ -254,12 +254,16 @@
     mean_high, mean_low = vectors[4].astype(bf16), vectors[5].astype(bf16)
     scale1, scale2 = vectors[6], vectors[7]
 
-    for y in range(SIDE):
+    def normalize(y):
         away = delta[pl.ds(y * ROW, ROW), :].astype(f32).reshape(SIDE, IMAGES, MID)
         reduced = jnp.maximum((away + offset1[None]) * scale1[None], 0.0)
         store_windows(windows, reduced.reshape(ROW, MID).astype(bf16), y)
 
+    normalize(0)
+
     for y in range(SIDE):
+        if y + 1 < SIDE:
+            normalize(y + 1)
         second = convolve_row(windows, spatial_weight, y).reshape(SIDE, IMAGES, MID)
         kept = jnp.maximum((second - center2[None]) * scale2[None], 0.0)
         spatial[pl.ds(y * ROW, ROW), :] = kept.reshape(ROW, MID).astype(bf16)
@@ -389,7 +393,7 @@
         scratch_shapes=[
             scratch(ROWS, MID, dtype=f32),
             scratch(ROWS + 2 * ROW, 3 * MID),
-            scratch(ROWS, MID),
+            scratch(OUT // MID, IMAGES, MID, dtype=f32),
         ],
         compiler_params=params(30),
         name="block",

time: 110 us -> 109 us (level)
  Pallas kernels: 41.6 us -> 40.4 us
where the time goes in v3:
time: 109 us; the launch traced here: 108 us
  blocking collectives  48.3 us (44%)
  Pallas kernels  40.4 us (37%)
  starting transfers between devices  10.3 us (9%)
  waiting for transfers between devices  7.64 us (7%)
  between operations  1.53 us (1%)
    all_to_all x1, blocking collectives, per_device(): lax.all_to_all(message, 'member', split_axis=0, concat_axis=0, tiled=True)  34.1 us
    all_to_all x1, blocking collectives, per_device(): lax.all_to_all(moments, 'member', split_axis=0, concat_axis=0, tiled=True)  14.2 us
    pallas_call x1, Pallas kernels, home_call(): pl.pallas_call(home_kernel, in_specs=[VMEM] * 9, out_specs=[VMEM, VMEM],...  13.5 us
    pallas_call x1, Pallas kernels, block_call(): pl.pallas_call(block_kernel, in_specs=[VMEM] * 3, out_specs=[VMEM, VMEM],...  12.8 us
    pallas_call x1, Pallas kernels, reduce_call(): pl.pallas_call(reduce_kernel, in_specs=[SMEM] + [HBM] * 6, out_specs=[VME...  7.1 us
    all_to_all x1, starting transfers between devices, per_device(): lax.all_to_all(copies, ('group', 'member'), split_axis=0, concat_axis=0,...  6.53 us
    all_to_all x1, waiting for transfers between devices, per_device(): lax.all_to_all(copies, ('group', 'member'), split_axis=0, concat_axis=0,...  6.11 us
    pallas_call x1, Pallas kernels, logits_call(): pl.pallas_call(logits_kernel, grid=(rows // step,), in_specs=[pl.BlockSpe...  4.7 us
  transfers between devices with their start and end apart: 2, of which 2 were waited for; matrix products, arithmetic and copies ran while one was open for 0% of the time, Pallas kernels for 4%

profile of v3, /device:TPU:1, one launch (start us, length us, event | category | flops | bytes accessed | tf_op | source)
XLA Modules:
  0.0 108.2 jit_solution(12641441143875954619)
XLA Ops:
  1.3 0.1 pad_add_fusion.place_ref
  1.4 7.1 %reduce.1 = (bf16[1568,2048]{1,0:T(8,128)(2,1)S(1)}, bf16[3,1536,512]{2,1,0:T(8,128)(2,1)S(1)}, bf16[512,2048]{1,0:T(8,128)(2,1)S(1)}, bf16[1568,512]{1,0:T(8,12...) custom-call(s32[4]{0:T(128)S(1)} %pad_add_fusion.place_ref, ...), custom_call_target="tpu_custom_call" | custom-call | tf_op jit(solution)/shard_map/reduce/pallas_call | solution.py:363
  8.5 34.1 %all_to_all.15.received = bf16[32,8,3712]{2,1,0:T(8,128)(2,1)S(1)} all-to-all(bf16[32,8,3712]{2,1,0:T(8,128)(2,1)S(1)} %get-tuple-element.18), channel_id=1, replica_groups=mesh['group'=4,'member'=32] {'member'}, dimensions={0} | all-to-all | bytes 3801088 | tf_op jit(solution)/shard_map/all_to_all | solution.py:474
  42.6 0.0 copy-start.1
  42.6 0.0 copy-start.2
  42.6 12.8 %block.1 = (bf16[32,8,768]{2,1,0:T(8,128)(2,1)S(1)}, bf16[1024,128]{1,0:T(8,128)(2,1)S(1)}) custom-call(bf16[32,8,3712]{2,1,0:T(8,128)(2,1)S(1)} %all_to_all.15.received, bf16[3,1536,512]{2,1,0:T(8,128)(2,1)S(1)} %get-tuple-element.19.spatial_weight, bf16[512,2048]{1,0:T(8,128)(2,1)S(1)} %get-tuple-element.20.expand_weight), custom_call_target="tpu_custom_call" | custom-call | tf_op jit(solution)/shard_map/block/pallas_call | solution.py:388
  55.4 14.2 %all_to_all.16.received = bf16[32,8,768]{2,1,0:T(8,128)(2,1)S(1)} all-to-all(bf16[32,8,768]{2,1,0:T(8,128)(2,1)S(1)} %get-tuple-element.21), channel_id=1, replica_groups=mesh['group'=4,'member'=32] {'member'}, dimensions={0} | all-to-all | bytes 786432 | tf_op jit(solution)/shard_map/all_to_all | solution.py:476
  69.6 0.0 copy-done.1
  69.6 0.0 copy-done.2
  69.6 0.0 copy-start
  69.6 13.5 %home.1 = (bf16[64,32,128]{2,1,0:T(8,128)(2,1)}, f32[1,32]{1,0:T(1,128)}) custom-call(bf16[32,8,768]{2,1,0:T(8,128)(2,1)S(1)} %all_to_all.16.received, bf16[32,32]{1,0:T(8,128)(2,1)S(1)} %get-tuple-element.22.select, bf16[32,512]{1,0:T(8,128)(2,1)S(1)} %get-tuple-element.23.mean, bf16[1568,512]{1,0:T(8,128)(2,1)S(1)} %get-tuple-element.24.delta, ...), custom_call_target="tpu_custom_call" | custom-call | tf_op jit(solution)/shard_map/home/pallas_call | solution.py:404
  83.1 6.5 %all-to-all-start.2 = ((bf16[64,32,128]{2,1,0:T(8,128)(2,1)}), bf16[64,32,128]{2,1,0:T(8,128)(2,1)S(1)}, u32[]{:S(2)}, u32[]{:S(2)}) async-start(bf16[64,32,128]{2,1,0:T(8,128)(2,1)} %get-tuple-element.28), calls=%async_computation.2 | async-start | bytes 1048576 | tf_op jit(solution)/shard_map/all_to_all | solution.py:483
  89.7 0.0 copy-done
  89.7 4.7 %logits.1 = bf16[1024,2048]{1,0:T(8,128)(2,1)} custom-call(bf16[1024,128]{1,0:T(8,128)(2,1)S(1)} %get-tuple-element.29.units_ref, bf16[2048,128]{1,0:T(8,128)(2,1)S(1)} %copy-done), custom_call_target="tpu_custom_call" | custom-call | flops 536870912 | bytes 4194304 | tf_op jit(solution)/shard_map/logits/pallas_call | solution.py:422
  94.4 6.1 %all-to-all-done.2 = bf16[64,32,128]{2,1,0:T(8,128)(2,1)S(1)} async-done(((bf16[64,32,128]{2,1,0:T(8,128)(2,1)}), bf16[64,32,128]{2,1,0:T(8,128)(2,1)S(1)}, u32[]{:S(2)}, u32[]{:S(2)}) %all-to-all-start.2) | async-done | bytes 524320 | tf_op jit(solution)/shard_map/all_to_all | solution.py:483
  100.5 3.7 %collective-permute-start = (bf16[64,32,128]{2,1,0:T(8,128)(2,1)S(1)}, bf16[64,32,128]{2,1,0:T(8,128)(2,1)S(1)}, u32[]{:S(2)}, u32[]{:S(2)}) collective-permute-start(bf16[64,32,128]{2,1,0:T(8,128)(2,1)S(1)} %all-to-all-done.2), channel_id=1, source_target_pairs={{0,32},{32,0},{64,96},{96,64},{1,33},{33,1},{65,97},{97,65},{2,34}... | collective-permute-start | bytes 1572872 | tf_op jit(solution)/shard_map/ppermute | solution.py:487
  104.2 1.5 %collective-permute-done = bf16[64,32,128]{2,1,0:T(8,128)(2,1)S(1)} collective-permute-done((bf16[64,32,128]{2,1,0:T(8,128)(2,1)S(1)}, bf16[64,32,128]{2,1,0:T(8,128)(2,1)S(1)}, u32[]{:S(2)}, u32[]{:S(2)}) %collective-permute-start) | collective-permute-done | bytes 524320 | tf_op jit(solution)/shard_map/ppermute | solution.py:487
  105.8 2.2 %queue.1 = bf16[2048,128]{1,0:T(8,128)(2,1)} custom-call(s32[4]{0:T(128)S(1)} %pad_add_fusion.place_ref, bf16[2048,128]{1,0:T(8,128)(2,1)S(1)} %bitcast.14, bf16[2048,128]{1,0:T(8,128)(2,1)S(1)} %bitcast.15, bf16[2048,128]{1,0:T(8,128)(2,1)S(1)} %copy-done), custom_call_target="tpu_custom_call" | custom-call | tf_op jit(solution)/shard_map/queue/pallas_call | solution.py:440
Async XLA Ops:
  42.6 27.0 %copy-start.1 = (bf16[2048,128]{1,0:T(8,128)(2,1)S(1)}, bf16[2048,128]{1,0:T(8,128)(2,1)}, u32[]{:S(2)}) copy-start(bf16[2048,128]{1,0:T(8,128)(2,1)} %head.1) | copy-start | bytes 1572868
  42.6 27.0 %copy-start.2 = (bf16[32,128]{1,0:T(8,128)(2,1)S(1)}, bf16[32,128]{1,0:T(8,128)(2,1)}, u32[]{:S(2)}) copy-start(bf16[32,128]{1,0:T(8,128)(2,1)} %query.1) | copy-start | bytes 24580
  69.6 20.1 %copy-start = (bf16[2048,128]{1,0:T(8,128)(2,1)S(1)}, bf16[2048,128]{1,0:T(8,128)(2,1)}, u32[]{:S(2)}) copy-start(bf16[2048,128]{1,0:T(8,128)(2,1)} %memory_hbm.1) | copy-start | bytes 1572868
  83.1 17.4 %all-to-all-start.2 = ((bf16[64,32,128]{2,1,0:T(8,128)(2,1)}), bf16[64,32,128]{2,1,0:T(8,128)(2,1)S(1)}, u32[]{:S(2)}, u32[]{:S(2)}) async-start(bf16[64,32,128]{2,1,0:T(8,128)(2,1)} %get-tuple-element.28), calls=%async_computation.2 | async-start | bytes 1048576 | tf_op jit(solution)/shard_map/all_to_all | solution.py:483
  100.5 5.3 %collective-permute-start = (bf16[64,32,128]{2,1,0:T(8,128)(2,1)S(1)}, bf16[64,32,128]{2,1,0:T(8,128)(2,1)S(1)}, u32[]{:S(2)}, u32[]{:S(2)}) collective-permute-start(bf16[64,32,128]{2,1,0:T(8,128)(2,1)S(1)} %all-to-all-done.2), channel_id=1, source_target_pairs={{0,32},{32,0},{64,96},{96,64},{1,33},{33,1},{65,97},{97,65},{2,34}... | collective-permute-start | bytes 1572872 | tf_op jit(solution)/shard_map/ppermute | solution.py:487

commit v4 on v3

--- a/solution.py
+++ b/solution.py
@@ -90,9 +90,12 @@
     return (chosen == iota((IMAGES, IMAGES), 1).astype(f32)).astype(bf16)
 
 
+WAITS = {0: (0,), 1: (1, 2), 3: (3, 4, 5, 6)}
+
+
 def reduce_kernel(
     place_ref, x_hbm, weight_hbm, table_hbm, query_hbm, spatial_hbm, expand_hbm,
-    x, spatial_weight, expand_weight, delta, mean_ref, select_ref, message,
+    x, spatial_weight, expand_weight, delta, mean_ref, back_ref, message,
     weight, table, query, sems,
 ):
     map_rows = [pl.ds(y * ROW, ROW) for y in range(SIDE)]
@@ -108,9 +111,9 @@
 
     loads[0].wait()
     loads[1].wait()
-    select = peer_selector(place_ref, table)
-    select_ref[...] = select
-    mover = spread_select(select)
+    mover = spread_select(peer_selector(place_ref, table))
+    same = (iota((SIZE, SIZE), 0) == iota((SIZE, SIZE), 1)).astype(bf16)
+    back_ref[...] = dot_tn(mover, same).astype(bf16)
     unit = unit_of(query[...])
     unit = jnp.concatenate([unit[SLAB * k : SLAB * (k + 1)] for k in range(4)], axis=1)
     message[:, :, pl.ds(QUERIES, MID)] = jnp.broadcast_to(unit[None], (IMAGES, SLAB, MID)).astype(bf16)
@@ -127,7 +130,7 @@
             done[0] += 1
 
     for y in range(SIDE):
-        for k in {0: [0], 1: [1, 2, 3], 4: [4, 5, 6]}.get(y, ()):
+        for k in WAITS.get(y, ()):
             loads[6 + k].wait()
         part = dot(x[map_rows[y], :], weight[...]).reshape(SIDE, IMAGES, MID)
         if y == 0:
@@ -239,11 +242,11 @@
 
 
 def home_kernel(
-    received, select, mean, delta, spatial_weight, expand_weight, x, head, query,
-    keys, similarity_ref, windows, spatial, pooled,
+    received, back, mean, delta, spatial_weight, expand_weight, x, head,
+    keys, windows, spatial, pooled,
 ):
     clear_border(windows)
-    stats = dot_tn(spread_select(select[...]), received[...].reshape(SIZE, MOMENTS))
+    stats = dot(back[...], received[...].reshape(SIZE, MOMENTS))
     stats = stats.reshape(SLAB, IMAGES, MOMENTS)
     vectors = []
     for k in range(12):
@@ -285,28 +288,22 @@
     key = projected * lax.rsqrt(jnp.sum(projected * projected, axis=1, keepdims=True) + unit_eps)
     key = key.astype(bf16)
     keys[...] = jnp.broadcast_to(key[None], keys.shape)
-    unit = unit_of(query[...]).astype(bf16)
-    pairs = dot_nt(unit, key)
-    own = iota((IMAGES, IMAGES), 0) == iota((IMAGES, IMAGES), 1)
-    similarity_ref[...] = jnp.sum(jnp.where(own, pairs, 0.0), axis=0, keepdims=True) / sharpness_divisor
 
 
 def logits_kernel(units_ref, memory_ref, out_ref):
     out_ref[...] = (dot_nt(units_ref[...], memory_ref[...]) * (1.0 / sharpness_divisor)).astype(bf16)
 
 
-def queue_kernel(place_ref, near_hbm, far_hbm, memory_hbm, out_ref, padded, memory, sems):
+def queue_kernel(place_ref, near_ref, far_ref, memory, out_hbm, padded, out_ref, sems):
     slots = memory.shape[0]
     batch = 4 * IMAGES * IMAGES
     half = IMAGES * IMAGES
     core = place_ref[2]
     start = place_ref[3]
-    pairs = [(memory_hbm, memory)]
     for high in range(2):
-        for ref, which in ((near_hbm, core), (far_hbm, 1 - core)):
+        for ref, which in ((near_ref, core), (far_ref, 1 - core)):
             at = pl.multiple_of(slots + (2 * high + which) * half, half)
-            pairs.append((ref.at[pl.ds(high * half, half), :], padded.at[pl.ds(at, half), :]))
-    loads = start_all(pairs, sems)
+            padded[pl.ds(at, half), :] = ref[pl.ds(high * half, half), :]
     edge = jnp.zeros((slots, KEY), bf16)
     padded[pl.ds(0, slots), :] = edge
     padded[pl.ds(slots + batch, slots), :] = edge
@@ -314,8 +311,7 @@
     base = start // ALIGN * ALIGN
     inner = start - base
     pick = (iota((TILE, TILE + ALIGN), 1) == iota((TILE, TILE + ALIGN), 0) + inner).astype(bf16)
-    for copy in loads:
-        copy.wait()
+    stores = []
     for part in range(slots // TILE):
         rows = padded[pl.ds(pl.multiple_of(base + part * TILE, ALIGN), TILE + ALIGN), :]
         fresh = dot(pick, rows)
@@ -323,10 +319,18 @@
         inside = jnp.logical_and(index >= 0, index < batch)
         old = memory[pl.ds(part * TILE, TILE), :].astype(f32)
         out_ref[pl.ds(part * TILE, TILE), :] = jnp.where(inside, fresh, old).astype(bf16)
-
-
+        if (part + 1) * TILE % STORE == 0:
+            rows = pl.ds((part + 1) * TILE - STORE, STORE)
+            store = pltpu.make_async_copy(out_ref.at[rows, :], out_hbm.at[rows, :], sems.at[len(stores)])
+            store.start()
+            stores.append(store)
+    for store in stores:
+        store.wait()
+
+
+STORE = 512
 ALIGN = 16
-TILE = 256
+TILE = 64
 
 
 def params(mib):
@@ -370,7 +374,7 @@
             scratch(MID, OUT),
             scratch(ROWS, MID),
             scratch(IMAGES, MID),
-            scratch(IMAGES, IMAGES),
+            scratch(SIZE, SIZE),
             scratch(IMAGES, SLAB, MESSAGE),
         ],
         scratch_shapes=[
@@ -400,12 +404,12 @@
     )(*in_vmem(received, spatial_weight, expand_weight))
 
 
-def home_call(received, select, mean, delta, spatial_weight, expand_weight, x, key_head, queries, copies):
+def home_call(received, back, mean, delta, spatial_weight, expand_weight, x, key_head, copies):
     return pl.pallas_call(
         home_kernel,
-        in_specs=[VMEM] * 9,
-        out_specs=[VMEM, VMEM],
-        out_shape=[scratch(copies, IMAGES, KEY), shape(1, IMAGES, dtype=f32)],
+        in_specs=[VMEM] * 8,
+        out_specs=VMEM,
+        out_shape=scratch(copies, IMAGES, KEY),
         scratch_shapes=[
             scratch(ROWS + 2 * ROW, 3 * MID),
             scratch(ROWS, MID),
@@ -413,7 +417,7 @@
         ],
         compiler_params=params(30),
         name="home",
-    )(*in_vmem(received, select, mean, delta, spatial_weight, expand_weight, x), key_head, queries)
+    )(*in_vmem(received, back, mean, delta, spatial_weight, expand_weight, x), key_head)
 
 
 def logits_call(units, memory):
@@ -436,20 +440,41 @@
     )(units, memory)
 
 
+def similarity_kernel(place_ref, keys, query, similarity_ref):
+    own_rows = (place_ref[0] // 2 * IMAGES + place_ref[1]) * IMAGES
+    key = keys[pl.ds(pl.multiple_of(own_rows, IMAGES), IMAGES), :]
+    pairs = dot_nt(unit_of(query[...]).astype(bf16), key)
+    own = iota((IMAGES, IMAGES), 0) == iota((IMAGES, IMAGES), 1)
+    similarity = jnp.sum(jnp.where(own, pairs, 0.0), axis=0, keepdims=True)
+    similarity_ref[...] = similarity / sharpness_divisor
+
+
+def similarity_call(place, near, queries):
+    return pl.pallas_call(
+        similarity_kernel,
+        in_specs=[SMEM, VMEM, VMEM],
+        out_specs=VMEM,
+        out_shape=shape(1, IMAGES, dtype=f32),
+        compiler_params=params(12),
+        cost_estimate=pl.CostEstimate(flops=MIB, bytes_accessed=MIB, transcendentals=0),
+        name="similarity",
+    )(place, *in_vmem(near.reshape(-1, KEY)), queries)
+
+
 def queue_call(place, near, far, memory):
     return pl.pallas_call(
         queue_kernel,
-        in_specs=[SMEM, ANY, ANY, ANY],
-        out_specs=VMEM,
+        in_specs=[SMEM, VMEM, VMEM, VMEM],
+        out_specs=ANY,
         out_shape=shape(*memory.shape),
         scratch_shapes=[
             scratch(2 * memory.shape[0] + 4 * IMAGES * IMAGES + ALIGN, KEY),
             scratch(*memory.shape),
-            dma(5),
+            dma(memory.shape[0] // STORE),
         ],
         compiler_params=params(32),
         name="queue",
-    )(place, near.reshape(-1, KEY), far.reshape(-1, KEY), memory)
+    )(place, *in_vmem(near.reshape(-1, KEY), far.reshape(-1, KEY)), memory)
 
 
 def per_device(
@@ -468,15 +493,13 @@
     x = activations.transpose(1, 2, 0, 3).reshape(ROWS, OUT)
     spatial_weight = conv_spatial.reshape(3, 3 * MID, MID)
     table = shuffle.reshape(batch // KEY, KEY)
-    x, spatial_weight, expand_weight, delta, mean, select, message = reduce_call(
+    x, spatial_weight, expand_weight, delta, mean, back, message = reduce_call(
         place, x, conv_reduce, table, queries, spatial_weight, conv_expand
     )
     received = lax.all_to_all(message, "member", split_axis=0, concat_axis=0, tiled=True)
     moments, units = block_call(received, spatial_weight, expand_weight)
     returned = lax.all_to_all(moments, "member", split_axis=0, concat_axis=0, tiled=True)
-    copies, similarity = home_call(
-        returned, select, mean, delta, spatial_weight, expand_weight, x, key_head, queries, 2 * members
-    )
+    copies = home_call(returned, back, mean, delta, spatial_weight, expand_weight, x, key_head, 2 * members)
     copies, units = lax.optimization_barrier((copies, units))
     logits = logits_call(units, negative_memory)
     same_core = [[g * members + m for g in (core, core + 2) for m in range(members)] for core in (0, 1)]
@@ -485,6 +508,7 @@
     )
     near, logits = lax.optimization_barrier((near, logits))
     far = lax.ppermute(near, "group", [(0, 1), (1, 0), (2, 3), (3, 2)])
+    similarity = similarity_call(place, near, queries)
     new_queue = queue_call(place, near, far, negative_memory)
     return logits, similarity.reshape(IMAGES), new_queue
 

time: 109 us -> 107 us (0.982)
  waiting for transfers between devices: 7.64 us -> 6.36 us
    ppermute x1, waiting for transfers between devices: 1.54 us -> 0.27 us  [per_device(): far = lax.ppermute(near, 'group', [(0, 1), (1, 0), (2, 3), (3, 2)])]
    pallas_call x2 -> x3, Pallas kernels: 15.7 us -> 15.9 us  [the longest x1 12.8 us: home_call(): pl.pallas_call(home_kernel, in_specs=[VMEM] * 8, out_specs=VMEM, out_shap...]
  transfers between devices with their start and end apart: 2 -> 2, of which waited for: 2 -> 2; matrix products, arithmetic and copies ran while one was open for 0% -> 0% of each run, Pallas kernels for 4% -> 6%
where the time goes in v4:
time: 107 us
  blocking collectives  48.3 us (45%)
  Pallas kernels  40.4 us (38%)
  starting transfers between devices  10.3 us (10%)
  waiting for transfers between devices  6.36 us (6%)
  between operations  1.54 us (1%)
    all_to_all x1, blocking collectives, per_device(): lax.all_to_all(message, 'member', split_axis=0, concat_axis=0, tiled=True)  34.1 us
    all_to_all x1, blocking collectives, per_device(): lax.all_to_all(moments, 'member', split_axis=0, concat_axis=0, tiled=True)  14.2 us
    pallas_call x1, Pallas kernels, block_call(): pl.pallas_call(block_kernel, in_specs=[VMEM] * 3, out_specs=[VMEM, VMEM],...  12.8 us
    pallas_call x1, Pallas kernels, home_call(): pl.pallas_call(home_kernel, in_specs=[VMEM] * 8, out_specs=VMEM, out_shap...  12.8 us
    pallas_call x1, Pallas kernels, reduce_call(): pl.pallas_call(reduce_kernel, in_specs=[SMEM] + [HBM] * 6, out_specs=[VME...  6.91 us
    all_to_all x1, starting transfers between devices, per_device(): lax.all_to_all(copies, ('group', 'member'), split_axis=0, concat_axis=0,...  6.55 us
    all_to_all x1, waiting for transfers between devices, per_device(): lax.all_to_all(copies, ('group', 'member'), split_axis=0, concat_axis=0,...  6.09 us
    pallas_call x1, Pallas kernels, logits_call(): pl.pallas_call(logits_kernel, grid=(rows // step,), in_specs=[pl.BlockSpe...  4.7 us
  transfers between devices with their start and end apart: 2, of which 2 were waited for; matrix products, arithmetic and copies ran while one was open for 0% of the time, Pallas kernels for 6%

profile of v4, /device:TPU:1, one launch (start us, length us, event | category | flops | bytes accessed | tf_op | source)
XLA Modules:
  0.0 106.9 jit_solution(9427178922749843034)
XLA Ops:
  1.3 0.1 pad_add_fusion.place_ref
  1.4 6.9 %reduce.1 = (bf16[1568,2048]{1,0:T(8,128)(2,1)S(1)}, bf16[3,1536,512]{2,1,0:T(8,128)(2,1)S(1)}, bf16[512,2048]{1,0:T(8,128)(2,1)S(1)}, bf16[1568,512]{1,0:T(8,12...) custom-call(s32[4]{0:T(128)S(1)} %pad_add_fusion.place_ref, ...), custom_call_target="tpu_custom_call" | custom-call | tf_op jit(solution)/shard_map/reduce/pallas_call | solution.py:367
  8.3 34.1 %all_to_all.15.received = bf16[32,8,3712]{2,1,0:T(8,128)(2,1)S(1)} all-to-all(bf16[32,8,3712]{2,1,0:T(8,128)(2,1)S(1)} %get-tuple-element.16), channel_id=1, replica_groups=mesh['group'=4,'member'=32] {'member'}, dimensions={0} | all-to-all | bytes 3801088 | tf_op jit(solution)/shard_map/all_to_all | solution.py:499
  42.4 0.0 copy-start.1
  42.4 12.8 %block.1 = (bf16[32,8,768]{2,1,0:T(8,128)(2,1)S(1)}, bf16[1024,128]{1,0:T(8,128)(2,1)S(1)}) custom-call(bf16[32,8,3712]{2,1,0:T(8,128)(2,1)S(1)} %all_to_all.15.received, bf16[3,1536,512]{2,1,0:T(8,128)(2,1)S(1)} %get-tuple-element.17.spatial_weight, bf16[512,2048]{1,0:T(8,128)(2,1)S(1)} %get-tuple-element.18.expand_weight), custom_call_target="tpu_custom_call" | custom-call | tf_op jit(solution)/shard_map/block/pallas_call | solution.py:392
  55.2 14.2 %all_to_all.16.received = bf16[32,8,768]{2,1,0:T(8,128)(2,1)S(1)} all-to-all(bf16[32,8,768]{2,1,0:T(8,128)(2,1)S(1)} %get-tuple-element.19), channel_id=1, replica_groups=mesh['group'=4,'member'=32] {'member'}, dimensions={0} | all-to-all | bytes 786432 | tf_op jit(solution)/shard_map/all_to_all | solution.py:501
  69.4 0.0 copy-done.1
  69.4 0.0 copy-start
  69.4 12.8 %home.1 = bf16[64,32,128]{2,1,0:T(8,128)(2,1)} custom-call(bf16[32,8,768]{2,1,0:T(8,128)(2,1)S(1)} %all_to_all.16.received, bf16[256,256]{1,0:T(8,128)(2,1)S(1)} %get-tuple-element.20.back, bf16[32,512]{1,0:T(8,128)(2,1)S(1)} %get-tuple-element.21.mean, bf16[1568,512]{1,0:T(8,128)(2,1)S(1)} %get-tuple-element.22.delta, ...), custom_call_target="tpu_custom_call" | custom-call | tf_op jit(solution)/shard_map/home/pallas_call | solution.py:408
  82.3 6.5 %all-to-all-start.2 = ((bf16[64,32,128]{2,1,0:T(8,128)(2,1)}), bf16[64,32,128]{2,1,0:T(8,128)(2,1)S(1)}, u32[]{:S(2)}, u32[]{:S(2)}) async-start(bf16[64,32,128]{2,1,0:T(8,128)(2,1)} %home.1), calls=%async_computation.2 | async-start | bytes 1048576 | tf_op jit(solution)/shard_map/all_to_all | solution.py:506
  88.8 0.0 copy-done
  88.8 0.0 copy-start.2
  88.8 4.7 %logits.1 = bf16[1024,2048]{1,0:T(8,128)(2,1)} custom-call(bf16[1024,128]{1,0:T(8,128)(2,1)S(1)} %get-tuple-element.26.units_ref, bf16[2048,128]{1,0:T(8,128)(2,1)S(1)} %copy-done), custom_call_target="tpu_custom_call" | custom-call | flops 536870912 | bytes 4194304 | tf_op jit(solution)/shard_map/logits/pallas_call | solution.py:426
  93.5 6.1 %all-to-all-done.2 = bf16[64,32,128]{2,1,0:T(8,128)(2,1)S(1)} async-done(((bf16[64,32,128]{2,1,0:T(8,128)(2,1)}), bf16[64,32,128]{2,1,0:T(8,128)(2,1)S(1)}, u32[]{:S(2)}, u32[]{:S(2)}) %all-to-all-start.2) | async-done | bytes 524320 | tf_op jit(solution)/shard_map/all_to_all | solution.py:506
  99.6 3.7 %collective-permute-start = (bf16[64,32,128]{2,1,0:T(8,128)(2,1)S(1)}, bf16[64,32,128]{2,1,0:T(8,128)(2,1)S(1)}, u32[]{:S(2)}, u32[]{:S(2)}) collective-permute-start(bf16[64,32,128]{2,1,0:T(8,128)(2,1)S(1)} %all-to-all-done.2), channel_id=1, source_target_pairs={{0,32},{32,0},{64,96},{96,64},{1,33},{33,1},{65,97},{97,65},{2,34}... | collective-permute-start | bytes 1572872 | tf_op jit(solution)/shard_map/ppermute | solution.py:510
  103.3 0.0 copy-done.2
  103.3 1.3 %similarity.1 = f32[1,32]{1,0:T(1,128)} custom-call(s32[4]{0:T(128)S(1)} %pad_add_fusion.place_ref, bf16[2048,128]{1,0:T(8,128)(2,1)S(1)} %bitcast.14, bf16[32,128]{1,0:T(8,128)(2,1)S(1)} %copy-done.2), custom_call_target="tpu_custom_call" | custom-call | flops 1048576 | bytes 1048576 | tf_op jit(solution)/shard_map/similarity/pallas_call | solution.py:453
  104.6 0.3 collective-permute-done
  104.9 1.8 %queue.1 = bf16[2048,128]{1,0:T(8,128)(2,1)} custom-call(s32[4]{0:T(128)S(1)} %pad_add_fusion.place_ref, bf16[2048,128]{1,0:T(8,128)(2,1)S(1)} %bitcast.15, bf16[2048,128]{1,0:T(8,128)(2,1)S(1)} %bitcast.16, bf16[2048,128]{1,0:T(8,128)(2,1)S(1)} %copy-done), custom_call_target="tpu_custom_call" | custom-call | tf_op jit(solution)/shard_map/queue/pallas_call | solution.py:465
Async XLA Ops:
  42.4 27.1 %copy-start.1 = (bf16[2048,128]{1,0:T(8,128)(2,1)S(1)}, bf16[2048,128]{1,0:T(8,128)(2,1)}, u32[]{:S(2)}) copy-start(bf16[2048,128]{1,0:T(8,128)(2,1)} %head.1) | copy-start | bytes 1572868
  69.4 19.4 %copy-start = (bf16[2048,128]{1,0:T(8,128)(2,1)S(1)}, bf16[2048,128]{1,0:T(8,128)(2,1)}, u32[]{:S(2)}) copy-start(bf16[2048,128]{1,0:T(8,128)(2,1)} %memory.1) | copy-start | bytes 1572868
  82.3 17.4 %all-to-all-start.2 = ((bf16[64,32,128]{2,1,0:T(8,128)(2,1)}), bf16[64,32,128]{2,1,0:T(8,128)(2,1)S(1)}, u32[]{:S(2)}, u32[]{:S(2)}) async-start(bf16[64,32,128]{2,1,0:T(8,128)(2,1)} %home.1), calls=%async_computation.2 | async-start | bytes 1048576 | tf_op jit(solution)/shard_map/all_to_all | solution.py:506
  88.8 14.5 %copy-start.2 = (bf16[32,128]{1,0:T(8,128)(2,1)S(1)}, bf16[32,128]{1,0:T(8,128)(2,1)}, u32[]{:S(2)}) copy-start(bf16[32,128]{1,0:T(8,128)(2,1)} %query.1) | copy-start | bytes 24580
  99.6 5.2 %collective-permute-start = (bf16[64,32,128]{2,1,0:T(8,128)(2,1)S(1)}, bf16[64,32,128]{2,1,0:T(8,128)(2,1)S(1)}, u32[]{:S(2)}, u32[]{:S(2)}) collective-permute-start(bf16[64,32,128]{2,1,0:T(8,128)(2,1)S(1)} %all-to-all-done.2), channel_id=1, source_target_pairs={{0,32},{32,0},{64,96},{96,64},{1,33},{33,1},{65,97},{97,65},{2,34}... | collective-permute-start | bytes 1572872 | tf_op jit(solution)/shard_map/ppermute | solution.py:510

commit v5 on v4

--- a/solution.py
+++ b/solution.py
@@ -300,32 +300,42 @@
     half = IMAGES * IMAGES
     core = place_ref[2]
     start = place_ref[3]
-    for high in range(2):
-        for ref, which in ((near_ref, core), (far_ref, 1 - core)):
-            at = pl.multiple_of(slots + (2 * high + which) * half, half)
-            padded[pl.ds(at, half), :] = ref[pl.ds(high * half, half), :]
-    edge = jnp.zeros((slots, KEY), bf16)
-    padded[pl.ds(0, slots), :] = edge
-    padded[pl.ds(slots + batch, slots), :] = edge
-    padded[pl.ds(2 * slots + batch, ALIGN), :] = edge[:ALIGN]
-    base = start // ALIGN * ALIGN
-    inner = start - base
-    pick = (iota((TILE, TILE + ALIGN), 1) == iota((TILE, TILE + ALIGN), 0) + inner).astype(bf16)
-    stores = []
-    for part in range(slots // TILE):
-        rows = padded[pl.ds(pl.multiple_of(base + part * TILE, ALIGN), TILE + ALIGN), :]
-        fresh = dot(pick, rows)
-        index = start - slots + part * TILE + iota((TILE, KEY), 0)
-        inside = jnp.logical_and(index >= 0, index < batch)
-        old = memory[pl.ds(part * TILE, TILE), :].astype(f32)
-        out_ref[pl.ds(part * TILE, TILE), :] = jnp.where(inside, fresh, old).astype(bf16)
-        if (part + 1) * TILE % STORE == 0:
-            rows = pl.ds((part + 1) * TILE - STORE, STORE)
-            store = pltpu.make_async_copy(out_ref.at[rows, :], out_hbm.at[rows, :], sems.at[len(stores)])
-            store.start()
-            stores.append(store)
-    for store in stores:
-        store.wait()
+    empty = start == slots + batch
+
+    @pl.when(empty)
+    def _():
+        keep = pltpu.make_async_copy(memory, out_hbm, sems.at[0])
+        keep.start()
+        keep.wait()
+
+    @pl.when(jnp.logical_not(empty))
+    def _():
+        for high in range(2):
+            for ref, which in ((near_ref, core), (far_ref, 1 - core)):
+                at = pl.multiple_of(slots + (2 * high + which) * half, half)
+                padded[pl.ds(at, half), :] = ref[pl.ds(high * half, half), :]
+        edge = jnp.zeros((slots, KEY), bf16)
+        padded[pl.ds(0, slots), :] = edge
+        padded[pl.ds(slots + batch, slots), :] = edge
+        padded[pl.ds(2 * slots + batch, ALIGN), :] = edge[:ALIGN]
+        base = start // ALIGN * ALIGN
+        inner = start - base
+        pick = (iota((TILE, TILE + ALIGN), 1) == iota((TILE, TILE + ALIGN), 0) + inner).astype(bf16)
+        stores = []
+        for part in range(slots // TILE):
+            rows = padded[pl.ds(pl.multiple_of(base + part * TILE, ALIGN), TILE + ALIGN), :]
+            fresh = dot(pick, rows)
+            index = start - slots + part * TILE + iota((TILE, KEY), 0)
+            inside = jnp.logical_and(index >= 0, index < batch)
+            old = memory[pl.ds(part * TILE, TILE), :].astype(f32)
+            out_ref[pl.ds(part * TILE, TILE), :] = jnp.where(inside, fresh, old).astype(bf16)
+            if (part + 1) * TILE % STORE == 0:
+                rows = pl.ds((part + 1) * TILE - STORE, STORE)
+                store = pltpu.make_async_copy(out_ref.at[rows, :], out_hbm.at[rows, :], sems.at[len(stores)])
+                store.start()
+                stores.append(store)
+        for store in stores:
+            store.wait()
 
 
 STORE = 512

time: 107 us -> 107 us (level)
  no operation moved by 1% of the time
where the time goes in v5:
time: 107 us; the launch traced here: 106 us
  blocking collectives  48.3 us (45%)
  Pallas kernels  39.9 us (37%)
  starting transfers between devices  10.3 us (10%)
  waiting for transfers between devices  6.36 us (6%)
  between operations  1.54 us (1%)
    all_to_all x1, blocking collectives, per_device(): lax.all_to_all(message, 'member', split_axis=0, concat_axis=0, tiled=True)  34.1 us
    all_to_all x1, blocking collectives, per_device(): lax.all_to_all(moments, 'member', split_axis=0, concat_axis=0, tiled=True)  14.2 us
    pallas_call x1, Pallas kernels, block_call(): pl.pallas_call(block_kernel, in_specs=[VMEM] * 3, out_specs=[VMEM, VMEM],...  12.8 us
    pallas_call x1, Pallas kernels, home_call(): pl.pallas_call(home_kernel, in_specs=[VMEM] * 8, out_specs=VMEM, out_shap...  12.8 us
    pallas_call x1, Pallas kernels, reduce_call(): pl.pallas_call(reduce_kernel, in_specs=[SMEM] + [HBM] * 6, out_specs=[VME...  6.91 us
    all_to_all x1, starting transfers between devices, per_device(): lax.all_to_all(copies, ('group', 'member'), split_axis=0, concat_axis=0,...  6.55 us
    all_to_all x1, waiting for transfers between devices, per_device(): lax.all_to_all(copies, ('group', 'member'), split_axis=0, concat_axis=0,...  6.09 us
    pallas_call x1, Pallas kernels, logits_call(): pl.pallas_call(logits_kernel, grid=(rows // step,), in_specs=[pl.BlockSpe...  4.7 us
  transfers between devices with their start and end apart: 2, of which 2 were waited for; matrix products, arithmetic and copies ran while one was open for 0% of the time, Pallas kernels for 6%

profile of v5, /device:TPU:1, one launch (start us, length us, event | category | flops | bytes accessed | tf_op | source)
XLA Modules:
  0.0 106.4 jit_solution(2795882583266826471)
XLA Ops:
  1.3 0.1 pad_add_fusion.place_ref
  1.4 6.9 %reduce.1 = (bf16[1568,2048]{1,0:T(8,128)(2,1)S(1)}, bf16[3,1536,512]{2,1,0:T(8,128)(2,1)S(1)}, bf16[512,2048]{1,0:T(8,128)(2,1)S(1)}, bf16[1568,512]{1,0:T(8,12...) custom-call(s32[4]{0:T(128)S(1)} %pad_add_fusion.place_ref, ...), custom_call_target="tpu_custom_call" | custom-call | tf_op jit(solution)/shard_map/reduce/pallas_call | solution.py:377
  8.3 34.1 %all_to_all.15.received = bf16[32,8,3712]{2,1,0:T(8,128)(2,1)S(1)} all-to-all(bf16[32,8,3712]{2,1,0:T(8,128)(2,1)S(1)} %get-tuple-element.16), channel_id=1, replica_groups=mesh['group'=4,'member'=32] {'member'}, dimensions={0} | all-to-all | bytes 3801088 | tf_op jit(solution)/shard_map/all_to_all | solution.py:509
  42.4 0.0 copy-start.1
  42.4 12.8 %block.1 = (bf16[32,8,768]{2,1,0:T(8,128)(2,1)S(1)}, bf16[1024,128]{1,0:T(8,128)(2,1)S(1)}) custom-call(bf16[32,8,3712]{2,1,0:T(8,128)(2,1)S(1)} %all_to_all.15.received, bf16[3,1536,512]{2,1,0:T(8,128)(2,1)S(1)} %get-tuple-element.17.spatial_weight, bf16[512,2048]{1,0:T(8,128)(2,1)S(1)} %get-tuple-element.18.expand_weight), custom_call_target="tpu_custom_call" | custom-call | tf_op jit(solution)/shard_map/block/pallas_call | solution.py:402
  55.2 14.2 %all_to_all.16.received = bf16[32,8,768]{2,1,0:T(8,128)(2,1)S(1)} all-to-all(bf16[32,8,768]{2,1,0:T(8,128)(2,1)S(1)} %get-tuple-element.19), channel_id=1, replica_groups=mesh['group'=4,'member'=32] {'member'}, dimensions={0} | all-to-all | bytes 786432 | tf_op jit(solution)/shard_map/all_to_all | solution.py:511
  69.4 0.0 copy-done.1
  69.4 0.0 copy-start
  69.4 12.8 %home.1 = bf16[64,32,128]{2,1,0:T(8,128)(2,1)} custom-call(bf16[32,8,768]{2,1,0:T(8,128)(2,1)S(1)} %all_to_all.16.received, bf16[256,256]{1,0:T(8,128)(2,1)S(1)} %get-tuple-element.20.back, bf16[32,512]{1,0:T(8,128)(2,1)S(1)} %get-tuple-element.21.mean, bf16[1568,512]{1,0:T(8,128)(2,1)S(1)} %get-tuple-element.22.delta, ...), custom_call_target="tpu_custom_call" | custom-call | tf_op jit(solution)/shard_map/home/pallas_call | solution.py:418
  82.3 6.5 %all-to-all-start.2 = ((bf16[64,32,128]{2,1,0:T(8,128)(2,1)}), bf16[64,32,128]{2,1,0:T(8,128)(2,1)S(1)}, u32[]{:S(2)}, u32[]{:S(2)}) async-start(bf16[64,32,128]{2,1,0:T(8,128)(2,1)} %home.1), calls=%async_computation.2 | async-start | bytes 1048576 | tf_op jit(solution)/shard_map/all_to_all | solution.py:516
  88.8 0.0 copy-done
  88.8 0.0 copy-start.2
  88.8 4.7 %logits.1 = bf16[1024,2048]{1,0:T(8,128)(2,1)} custom-call(bf16[1024,128]{1,0:T(8,128)(2,1)S(1)} %get-tuple-element.26.units_ref, bf16[2048,128]{1,0:T(8,128)(2,1)S(1)} %copy-done), custom_call_target="tpu_custom_call" | custom-call | flops 536870912 | bytes 4194304 | tf_op jit(solution)/shard_map/logits/pallas_call | solution.py:436
  93.5 6.1 %all-to-all-done.2 = bf16[64,32,128]{2,1,0:T(8,128)(2,1)S(1)} async-done(((bf16[64,32,128]{2,1,0:T(8,128)(2,1)}), bf16[64,32,128]{2,1,0:T(8,128)(2,1)S(1)}, u32[]{:S(2)}, u32[]{:S(2)}) %all-to-all-start.2) | async-done | bytes 524320 | tf_op jit(solution)/shard_map/all_to_all | solution.py:516
  99.6 3.7 %collective-permute-start = (bf16[64,32,128]{2,1,0:T(8,128)(2,1)S(1)}, bf16[64,32,128]{2,1,0:T(8,128)(2,1)S(1)}, u32[]{:S(2)}, u32[]{:S(2)}) collective-permute-start(bf16[64,32,128]{2,1,0:T(8,128)(2,1)S(1)} %all-to-all-done.2), channel_id=1, source_target_pairs={{0,32},{32,0},{64,96},{96,64},{1,33},{33,1},{65,97},{97,65},{2,34}... | collective-permute-start | bytes 1572872 | tf_op jit(solution)/shard_map/ppermute | solution.py:520
  103.3 0.0 copy-done.2
  103.3 1.3 %similarity.1 = f32[1,32]{1,0:T(1,128)} custom-call(s32[4]{0:T(128)S(1)} %pad_add_fusion.place_ref, bf16[2048,128]{1,0:T(8,128)(2,1)S(1)} %bitcast.14, bf16[32,128]{1,0:T(8,128)(2,1)S(1)} %copy-done.2), custom_call_target="tpu_custom_call" | custom-call | flops 1048576 | bytes 1048576 | tf_op jit(solution)/shard_map/similarity/pallas_call | solution.py:463
  104.6 0.3 collective-permute-done
  104.9 1.4 %queue.1 = bf16[2048,128]{1,0:T(8,128)(2,1)} custom-call(s32[4]{0:T(128)S(1)} %pad_add_fusion.place_ref, bf16[2048,128]{1,0:T(8,128)(2,1)S(1)} %bitcast.15, bf16[2048,128]{1,0:T(8,128)(2,1)S(1)} %bitcast.16, bf16[2048,128]{1,0:T(8,128)(2,1)S(1)} %copy-done), custom_call_target="tpu_custom_call" | custom-call | tf_op jit(solution)/shard_map/queue/pallas_call | solution.py:475
Async XLA Ops:
  42.4 27.1 %copy-start.1 = (bf16[2048,128]{1,0:T(8,128)(2,1)S(1)}, bf16[2048,128]{1,0:T(8,128)(2,1)}, u32[]{:S(2)}) copy-start(bf16[2048,128]{1,0:T(8,128)(2,1)} %head.1) | copy-start | bytes 1572868
  69.4 19.4 %copy-start = (bf16[2048,128]{1,0:T(8,128)(2,1)S(1)}, bf16[2048,128]{1,0:T(8,128)(2,1)}, u32[]{:S(2)}) copy-start(bf16[2048,128]{1,0:T(8,128)(2,1)} %memory.1) | copy-start | bytes 1572868
  82.3 17.4 %all-to-all-start.2 = ((bf16[64,32,128]{2,1,0:T(8,128)(2,1)}), bf16[64,32,128]{2,1,0:T(8,128)(2,1)S(1)}, u32[]{:S(2)}, u32[]{:S(2)}) async-start(bf16[64,32,128]{2,1,0:T(8,128)(2,1)} %home.1), calls=%async_computation.2 | async-start | bytes 1048576 | tf_op jit(solution)/shard_map/all_to_all | solution.py:516
  88.8 14.5 %copy-start.2 = (bf16[32,128]{1,0:T(8,128)(2,1)S(1)}, bf16[32,128]{1,0:T(8,128)(2,1)}, u32[]{:S(2)}) copy-start(bf16[32,128]{1,0:T(8,128)(2,1)} %query.1) | copy-start | bytes 24580
  99.6 5.2 %collective-permute-start = (bf16[64,32,128]{2,1,0:T(8,128)(2,1)S(1)}, bf16[64,32,128]{2,1,0:T(8,128)(2,1)S(1)}, u32[]{:S(2)}, u32[]{:S(2)}) collective-permute-start(bf16[64,32,128]{2,1,0:T(8,128)(2,1)S(1)} %all-to-all-done.2), channel_id=1, source_target_pairs={{0,32},{32,0},{64,96},{96,64},{1,33},{33,1},{65,97},{97,65},{2,34}... | collective-permute-start | bytes 1572872 | tf_op jit(solution)/shard_map/ppermute | solution.py:520
